TPU v7x, 128 devices: a whole 4x4x4 slice. The times are simulated.
128 devices in a mesh: seq: 32 (over x, y, core), head: 4 (over z).
Axes of the slice: x: 4, y: 4, z: 4, core: 2. Of those that a mesh axis runs over, the one named last changes fastest.
Arguments:
- layer_in: bfloat16 [16384, 2048], P('seq', 'head'), may hold values from -6 to 6
- gain1: float32 [2048], replicated, may hold values from 0.25 to 1.75
- wq: bfloat16 [2048, 2048], P(None, 'head'), may hold values from -0.125 to 0.125
- wk: bfloat16 [2048, 2048], P(None, 'head'), may hold values from -0.125 to 0.125
- wv: bfloat16 [2048, 4096], P(None, 'head'), may hold values from -0.125 to 0.125
- wg: bfloat16 [2048, 4096], P(None, 'head'), may hold values from -0.125 to 0.125
- wo: bfloat16 [4096, 2048], P('head'), may hold values from -0.125 to 0.125
- gain2: float32 [2048], replicated, may hold values from 0.25 to 1.75
- w1: bfloat16 [2048, 4096], P(None, 'head'), may hold values from -0.125 to 0.125
- w2: bfloat16 [4096, 2048], P('head'), may hold values from -0.125 to 0.125
- starts: int32 [3], replicated, may hold values from 0 to 16383, as said below
- cotangent: bfloat16 [16384, 2048], P('seq', 'head'), may hold values from -6 to 6
Outputs:
- out: bfloat16 [16384, 2048], P('seq', 'head')
- grad_x: float32 [16384, 2048], P('seq', 'head')
- grad_gain1: float32 [2048], P('head')
- grad_wq: float32 [2048, 2048], P('seq', 'head')
- grad_wk: float32 [2048, 2048], P('seq', 'head')
- grad_wv: float32 [2048, 4096], P('seq', 'head')
- grad_wg: float32 [2048, 4096], P('seq', 'head')
- grad_wo: float32 [4096, 2048], P('head', 'seq')
- grad_gain2: float32 [2048], P('head')
- grad_w1: float32 [2048, 4096], P('seq', 'head')
- grad_w2: float32 [4096, 2048], P('head', 'seq')
Inputs may be any that keep to these rules, and one draw needn't show every extreme that they name: starts[0] = 0 and the starts rise strictly; starts[1] and starts[2] each lie in the first 512 tokens or in the last 512 tokens, so that one document holds tokens of both.
All inputs are finite; a program needn't handle non-finite values.
Results may differ from a plain program's by a relative error of at most 0.023.
Values may be sent and summed in bfloat16 or wider, within the bound.
No kernel may reach another device: no remote copies, remote signals or barrier semaphores. Data moves between devices by JAX's collectives and lax.ppermute only.
A program may use at most 256 MiB of HBM per device.

v0:
```python
import math

import jax
import jax.numpy as jnp
from jax import lax
from jax.experimental import pallas as pl
from jax.experimental.pallas import tpu as pltpu
from jax.sharding import PartitionSpec as P

KEY = 256
VAL = 512
SIDE = 4
CORES = 2
HEADS = 2
ROWS = 512
HALF = 256
PART = 512
MODEL = 2048
EXTRA = 16
EPSILON = 1e-05
F32 = jnp.float32
BF16 = jnp.bfloat16
VMEM_BYTES = 26 * 1024 * 1024
ORDER = (2, 1, 3, 0)


def head_shift(step):
    return [(h, (h + step) % SIDE) for h in range(SIDE)]


def seq_index(x, y, core):
    return (x * SIDE + y) * CORES + core


def seq_shift(dx, dy, swap=0):
    return [
        (seq_index(x, y, core), seq_index((x + dx) % SIDE, (y + dy) % SIDE, core ^ swap))
        for x in range(SIDE)
        for y in range(SIDE)
        for core in range(CORES)
    ]


SWAP = seq_shift(0, 0, 1)


def up(block):
    return lax.ppermute(block, "head", head_shift(1))


def down(block):
    return lax.ppermute(block, "head", head_shift(SIDE - 1))


def add_low(a, b):
    return (a.astype(F32) + b.astype(F32)).astype(BF16)


def relay(a, b, tokens):
    def body(a, b, to_a, to_b):
        to_a[...] = a[...]
        to_b[...] = b[...]

    return call(
        "relay", body, (1,), [], [(a,), (b,)], [(a.shape, a.dtype), (b.shape, b.dtype)], tokens
    )


def gated(array, tokens):
    n = len(tokens)

    def body(*refs):
        del refs

    out = pl.pallas_call(
        body,
        name="gated",
        in_specs=[pl.BlockSpec(memory_space=pl.ANY)] * (1 + n),
        out_specs=pl.BlockSpec(memory_space=pl.ANY),
        out_shape=pltpu.HBM(array.shape, array.dtype),
        input_output_aliases={0: 0},
    )(in_hbm(array), *[in_hbm(t) if is_pinned(t) else t for t in tokens])
    pin(out)
    return out


def hold(tokens):
    def body(out):
        out[...] = jnp.zeros_like(out)

    return call("hold", body, (1,), [], [], [((8, 128), F32)], tokens)[0]


def gather_direct(block):
    got = {k: lax.ppermute(block, "head", head_shift(k)) for k in (2, 1, 3)}
    return [block, got[1], got[2], got[3]]


def ring_gather(a, b, first=None):
    r1, l1 = up(a), down(b)
    r2, l2 = up(b), down(a)
    on_r, on_l = first(r1, l1) if first else (r1, l1)
    r3, l3 = up(on_r), down(on_l)
    return [a, b, r1, r2, r3, l3, l2, l1]


def ring_scatter(p2a, p2b, p1a, p1b, pma, pmb):
    t1, t2 = up(p2a), down(p2b)
    rb, la = up(p1b), down(pma)
    s1, s2 = add_low(p1a, t1), add_low(pmb, t2)
    ra, lb = up(s1), down(s2)
    return [ra, rb, la, lb], (s1, s2)


def whole(shape):
    return pl.BlockSpec(shape, lambda *_: (0,) * len(shape))


def once(shape):
    return pl.BlockSpec(
        shape, lambda *_: (0,) * len(shape), pipeline_mode=pl.Buffered(buffer_count=1)
    )


PINNED = []


def pin(*arrays):
    PINNED.extend(arrays)


def is_pinned(array):
    return any(array is other for other in PINNED)


def in_hbm(array):
    return pltpu.with_memory_space_constraint(array, pltpu.HBM)


COST_SCALE = 1.0
COSTS = {
    "kv_mid": 100,
    "scan_start_b": 100,
    "relay": 1,
    "hold": 0.1,
    "turn_low2": 1.5,
    "late": 100,
    "scan_end_b": 50,
    "norm1": 5,
    "key_value": 8,
    "query_part": 6,
    "gate": 4,
    "mix": 9,
    "cot_pass": 100,
    "feed_up": 11,
    "back_feed": 7,
    "back_mix": 6,
    "retain_back": 0.6,
    "feed_down": 2,
    "key_value_back": 100,
    "back_proj": 0.1,
    "feed_other": 5,
    "feed_own": 8,
    "mix_other": 0.180,
    "mix_own": 1,
    "kv_other": 0.90,
    "kv_own": 0.1,
    "feed_sum": 0.1,
    "mix_sum": 2,
    "kv_sum": 0.1,
    "norm_back1": 0.1,
    "norm_back2": 100,
}


def call(name, body, grid, scalars, ins, outs, tokens=(), scratch=(), keep=False):
    arrays = [in_hbm(item[0]) if is_pinned(item[0]) else item[0] for item in ins]
    in_specs = [once(i[0].shape) if len(i) == 1 else pl.BlockSpec(i[1], i[2]) for i in ins]
    out_specs = [whole(o[0]) if len(o) == 2 else pl.BlockSpec(o[2], o[3]) for o in outs]
    out_shape = [jax.ShapeDtypeStruct(o[0], o[1]) for o in outs]
    keep = range(len(outs)) if keep is True else (keep or ())
    out_shape = [
        pltpu.HBM(o.shape, o.dtype) if i in keep else o for i, o in enumerate(out_shape)
    ]
    n_in, n_tok, n_sc = len(arrays), len(tokens), len(scalars)
    tokens = [in_hbm(t) if is_pinned(t) else t for t in tokens]
    in_specs += [pl.BlockSpec(memory_space=pl.ANY)] * n_tok

    def run(*refs):
        body(*refs[: n_sc + n_in], *refs[n_sc + n_in + n_tok :])

    results = pl.pallas_call(
        run,
        name=name,
        grid_spec=pltpu.PrefetchScalarGridSpec(
            num_scalar_prefetch=n_sc,
            grid=grid,
            in_specs=in_specs,
            out_specs=out_specs,
            scratch_shapes=list(scratch),
        ),
        out_shape=out_shape,
        compiler_params=pltpu.CompilerParams(
            dimension_semantics=("arbitrary",) * len(grid), vmem_limit_bytes=VMEM_BYTES
        ),
        cost_estimate=pl.CostEstimate(
            flops=int(COSTS.get(name, 0.1) * COST_SCALE * 1.1e9),
            bytes_accessed=0,
            transcendentals=0,
        ),
    )(*scalars, *arrays, *tokens)
    pin(*[results[i] for i in keep])
    return results


def dot(left, right):
    return jnp.dot(left, right, preferred_element_type=F32)


def dot_t(left, right):
    return lax.dot_general(left, right, (((1,), (1,)), ((), ())), preferred_element_type=F32)


def t_dot(left, right):
    return lax.dot_general(left, right, (((0,), (0,)), ((), ())), preferred_element_type=F32)


def rotate(rows, cosine, sine):
    half = rows.shape[-1] // 2
    first, second = rows[:, :half], rows[:, half:]
    return jnp.concatenate([first * cosine - second * sine, second * cosine + first * sine], axis=1)


def sigmoid(v):
    return 0.5 + 0.5 * jnp.tanh(0.5 * v)


def head_col(info, k):
    return pl.multiple_of(lax.rem(info[0] + SIDE - k, SIDE) * PART, PART)


CHUNK = 16


def norm_rows(info, load, gain, low, mean_ref, inv_ref, own=None):
    for half in range(2):

        def step(i, _):
            at = pl.multiple_of(i * CHUNK, CHUNK)
            out = pl.ds(pl.multiple_of(half * HALF + i * CHUNK, CHUNK), CHUNK)
            parts = [load(k, half, at) for k in range(SIDE)]
            if own is not None:
                own[out, :] = parts[0]
            mean = sum(jnp.sum(p, axis=1, keepdims=True) for p in parts) / MODEL
            parts = [p - mean for p in parts]
            var = sum(jnp.sum(p * p, axis=1, keepdims=True) for p in parts) / MODEL
            inv = lax.rsqrt(var + EPSILON)
            mean_ref[out, :] = mean
            inv_ref[out, :] = inv
            for k in range(SIDE):
                cols = pl.ds(head_col(info, k), PART)
                low[out, cols] = (parts[k] * inv * gain[:, cols]).astype(BF16)
            return 0

        lax.fori_loop(0, HALF // CHUNK, step, 0, unroll=8)


def chunk_of(part, half, at):
    return part[pl.ds(pl.multiple_of(half * HALF + at, CHUNK), CHUNK), :].astype(F32)


def norm1(info, parts, gain, cotangent):
    def body(info, *refs):
        x = refs[:8]
        gain, cot, low, mean, inv, cot_out, rows = refs[8:]
        cot_out[...] = cot[...]
        for k in range(SIDE):
            rows[k, :HALF] = x[2 * k][...]
            rows[k, HALF:] = x[2 * k + 1][...]
        norm_rows(
            info,
            lambda k, half, at: x[2 * k + half][pl.ds(at, CHUNK), :].astype(F32),
            gain,
            low,
            mean,
            inv,
        )

    return call(
        "norm1",
        body,
        (1,),
        [info],
        [(p,) for p in parts] + [(gain,), (cotangent,)],
        [
            ((ROWS, MODEL), BF16),
            ((ROWS, 1), F32),
            ((ROWS, 1), F32),
            ((ROWS, PART), BF16),
            ((SIDE, ROWS, PART), BF16),
        ],
        keep=(4,),
    )


def key_value(info, low, wk, wv, cosine, sine, departure):
    def body(info, low, wk, wv, cosine, sine, departure, key, value, own, give):
        head = pl.program_id(0)
        k = rotate(dot(low[...], wk[...]), cosine[...], sine[...]).astype(BF16)
        key[...] = k
        v = dot(low[...], wv[...]).astype(BF16)
        value[...] = v
        state = t_dot((k.astype(F32) * departure[0]).astype(BF16), v)

        @pl.when(head == info[1])
        def _():
            own[...] = state

        @pl.when(head != info[1])
        def _():
            give[...] = state.astype(BF16)

    by_head = lambda h, *_: (0, h)
    return call(
        "key_value",
        body,
        (HEADS,),
        [info],
        [
            (low,),
            (wk, (MODEL, KEY), by_head),
            (wv, (MODEL, VAL), by_head),
            (cosine,),
            (sine,),
            (departure, (1, ROWS, 1), lambda h, *_: (h, 0, 0)),
        ],
        [
            ((ROWS, HEADS * KEY), BF16, (ROWS, KEY), by_head),
            ((ROWS, HEADS * VAL), BF16, (ROWS, VAL), by_head),
            ((KEY, VAL), F32),
            ((KEY, VAL), BF16),
        ],
        keep=(0, 1),
    )


def query_part(low, wq, key, value, decay, cosine, sine, tokens):
    def body(low, wq, key, value, decay, cosine, sine, query, weighted, within):
        q = rotate(dot(low[...], wq[...]), cosine[...], sine[...]).astype(BF16)
        query[...] = q
        w = (dot_t(q, key[...]) * decay[0]).astype(BF16)
        weighted[0] = w
        within[...] = dot(w, value[...])

    by_head = lambda h, *_: (0, h)
    cube = lambda h, *_: (h, 0, 0)
    return call(
        "query_part",
        body,
        (HEADS,),
        [],
        [
            (low,),
            (wq, (MODEL, KEY), by_head),
            (key, (ROWS, KEY), by_head),
            (value, (ROWS, VAL), by_head),
            (decay, (1, ROWS, ROWS), cube),
            (cosine,),
            (sine,),
        ],
        [
            ((ROWS, HEADS * KEY), BF16, (ROWS, KEY), by_head),
            ((HEADS, ROWS, ROWS), BF16, (1, ROWS, ROWS), cube),
            ((ROWS, HEADS * VAL), F32, (ROWS, VAL), by_head),
        ],
        tokens,
        keep=(0, 1),
    )


def matmul_cols(name, left, right, out_type, tokens=(), block=512):
    def body(left, right, out):
        out[...] = dot(left[...], right[...]).astype(out_type)

    depth, cols = right.shape
    by_col = lambda i, *_: (0, i)
    return call(
        name,
        body,
        (cols // block,),
        [],
        [(left,), (right, (depth, block), by_col)],
        [((left.shape[0], cols), out_type, (left.shape[0], block), by_col)],
        tokens,
        keep=True,
    )[0]


def block_outs(extra):
    tall = ((HALF + extra, PART), BF16)
    return [tall, ((HALF, PART), BF16)] * 3 + [((ROWS, PART), F32)]


def put_blocks(step, make, outs):
    for i in range(2):
        block = make(i)
        for s in range(2):
            k = 2 * s + i

            @pl.when(step == s)
            def _():
                if k == SIDE - 1:
                    outs[6][...] = block
                else:
                    outs[2 * k][:HALF, :] = block[:HALF].astype(BF16)
                    outs[2 * k + 1][...] = block[HALF:].astype(BF16)


def pick(mine, sibling, info, head):
    return jnp.where(info[1] == head, mine[...], sibling[...])


def mix(info, within, gate, query, mine, sibling, arrival, wo, tokens):
    def body(info, within, gate, query, mine, sibling, arrival, wo, mixed, grouped, ginv, *outs):
        for half in range(2):
            rows = slice(half * HALF, (half + 1) * HALF)
            for head in range(HEADS):
                cols = slice(head * VAL, (head + 1) * VAL)
                state = pick(mine, sibling, info, head)
                cross = dot(query[rows, head * KEY : (head + 1) * KEY], state)
                kept = within[rows, cols] + arrival[head, rows] * cross
                kept = kept - jnp.mean(kept, axis=1, keepdims=True)
                inv = lax.rsqrt(jnp.mean(kept * kept, axis=1, keepdims=True) + float(KEY))
                group = kept * inv
                g = gate[rows, cols].astype(F32)
                ginv[head, rows] = inv
                grouped[rows, cols] = group.astype(BF16)
                mixed[rows, cols] = (group * (g * sigmoid(g))).astype(BF16)
            for i in range(SIDE):
                at = pl.ds(pl.multiple_of(info[2 + i] * PART, PART), PART)
                block = dot(mixed[rows], wo[:, at])
                if i == SIDE - 1:
                    outs[6][rows] = block
                else:
                    outs[2 * i + half][...] = block.astype(BF16)

    cols = HEADS * VAL
    return call(
        "mix",
        body,
        (1,),
        [info],
        [(within,), (gate,), (query,), (mine,), (sibling,), (arrival,), (wo,)],
        [((ROWS, cols), BF16), ((ROWS, cols), BF16), ((HEADS, ROWS, 1), F32)] + block_outs(0),
        tokens,
        keep=(0, 1),
    )


def sum_branch(p0, pieces, tokens):
    def body(p0, ra, rb, la, lb, a, b):
        a[...] = (p0[:HALF] + ra[...].astype(F32) + la[...].astype(F32)).astype(BF16)
        b[...] = (p0[HALF:] + rb[...].astype(F32) + lb[...].astype(F32)).astype(BF16)

    return call(
        "sum_branch",
        body,
        (1,),
        [],
        [(p0,)] + [(p,) for p in pieces],
        [((HALF, PART), BF16), ((HALF, PART), BF16)],
        tokens,
    )


def feed_up(info, x_rows, b_parts, gain, w1, grad_hidden, tokens):
    block = 512

    def body(info, *refs):
        x, b = refs[0], refs[1:9]
        gain, w1, grad_hidden, ffn_in, mean, inv, own, hidden, grad_pre = refs[9:]

        @pl.when(pl.program_id(0) == 0)
        def _():
            def load(k, half, at):
                branch = b[2 * k + half][pl.ds(at, CHUNK), :].astype(F32)
                return chunk_of(x.at[k], half, at) + branch

            norm_rows(info, load, gain, ffn_in, mean, inv, own)

        pre = dot(ffn_in[...], w1[...])
        cdf = 0.5 * (1.0 + lax.erf(pre * (2.0**-0.5)))
        hidden[...] = (pre * cdf).astype(BF16)
        pdf = jnp.exp(-0.5 * pre * pre) * ((2.0 * math.pi) ** -0.5)
        grad_pre[...] = ((cdf + pre * pdf) * grad_hidden[...].astype(F32)).astype(BF16)

    by_col = lambda i, *_: (0, i)
    cols = w1.shape[1]
    tall = ((ROWS, cols), BF16, (ROWS, block), by_col)
    return call(
        "feed_up",
        body,
        (cols // block,),
        [info],
        [(x_rows,)]
        + [(p,) for p in b_parts]
        + [
            (gain,),
            (w1, (MODEL, block), by_col),
            (grad_hidden, (ROWS, block), by_col),
        ],
        [
            ((ROWS, MODEL), BF16),
            ((ROWS, 1), F32),
            ((ROWS, 1), F32),
            ((ROWS, PART), F32),
            tall,
            tall,
        ],
        tokens,
        keep=(1, 2, 3),
    )


def back_blocks(name, info, pairs, gain, low, tokens=()):
    n = len(pairs)

    def body(info, *refs):
        grads, weights = refs[:n], refs[n : 3 * n]
        gains, lows = refs[3 * n : 3 * n + 2], refs[3 * n + 2 : 3 * n + 4]
        outs, sums, acc = refs[3 * n + 4 : 3 * n + 11], refs[3 * n + 11], refs[3 * n + 12]
        step = pl.program_id(0)
        lane = lax.broadcasted_iota(jnp.int32, (ROWS, 128), 1)

        @pl.when(step == 0)
        def _():
            acc[...] = jnp.zeros_like(acc)

        def make(i):
            total = dot_t(grads[0][...], weights[2 * 0 + i][...])
            for j in range(1, n):
                total = total + dot_t(grads[j][...], weights[2 * j + i][...])
            first = jnp.sum(total * gains[i][...], axis=1, keepdims=True) / MODEL
            second = jnp.sum(total * lows[i][...].astype(F32), axis=1, keepdims=True) / MODEL
            acc[...] += jnp.where(lane == 0, first, jnp.where(lane == 1, second, 0.0))
            return total

        put_blocks(step, make, outs)

        @pl.when(step == 1)
        def _():
            turned = acc[...].T[:EXTRA]
            sums[...] = turned
            for k in range(SIDE - 1):
                outs[2 * k][HALF:, :] = turned.astype(BF16)

    def by_row(j):
        return lambda i, info: (info[2 + j + 2 * i], 0)

    def by_col(j):
        return lambda i, info: (0, info[2 + j + 2 * i])

    return call(
        name,
        body,
        (2,),
        [info],
        [(g,) for g, _ in pairs]
        + [(w, (PART, w.shape[1]), by_row(j)) for _, w in pairs for j in range(2)]
        + [(gain, (1, PART), by_col(j)) for j in range(2)]
        + [(low, (ROWS, PART), by_col(j)) for j in range(2)],
        block_outs(EXTRA) + [((EXTRA, PART), F32)],
        tokens,
        [pltpu.VMEM((ROWS, 128), F32)],
        keep=(6,),
    )


def norm_back(
    name, info, p0, sums, pieces, gain, rows, mean, inv, residual, low_out, tokens
):
    def body(
        info, p0, sums, ra, rb, la, lb, gain, rows, mean, inv, residual, grad, gain_grad, *low
    ):
        scale = gain[:, pl.ds(head_col(info, 0), PART)]
        total = sums[...] + ra[HALF:].astype(F32) + la[HALF:].astype(F32)
        total = jnp.concatenate([total, jnp.zeros((128 - EXTRA, PART), F32)], axis=0).T
        acc = jnp.zeros((1, PART), F32)
        for half, (one, two) in enumerate(((ra, la), (rb, lb))):
            for quarter in range(2):
                at = slice(quarter * 128, (quarter + 1) * 128)
                out = slice(half * HALF + quarter * 128, half * HALF + (quarter + 1) * 128)
                g = p0[out] + one[at].astype(F32) + two[at].astype(F32)
                normed = (rows[out].astype(F32) - mean[out]) * inv[out]
                acc = acc + jnp.sum(g * normed, axis=0, keepdims=True)
                back = inv[out] * (g * scale - total[out, 0:1] - normed * total[out, 1:2])
                new = residual[out].astype(F32) + back
                grad[out] = new
                if low_out:
                    low[half][at] = new.astype(BF16)
        gain_grad[...] = acc

    outs = [((ROWS, PART), F32), ((1, PART), F32)]
    if low_out:
        outs += [((HALF, PART), BF16)] * 2
    return call(
        name,
        body,
        (1,),
        [info],
        [(p0,), (sums,)]
        + [(p,) for p in pieces]
        + [(gain,), (rows,), (mean,), (inv,), (residual,)],
        outs,
        tokens,
        keep=(0,) if low_out else (),
    )


def back_mix(info, parts, wo, gate, grouped, ginv, query, arrival, tokens):
    def body(info, *refs):
        parts = refs[:8]
        wo, gate, grouped, ginv, query, arrival, branch, grad_gate, kept, own, give = refs[8:]
        head = pl.program_id(0)

        @pl.when(head == 0)
        def _():
            for k in range(SIDE):
                cols = pl.ds(head_col(info, k), PART)
                branch[:HALF, cols] = parts[2 * k][...]
                branch[HALF:, cols] = parts[2 * k + 1][...]

        for half in range(2):
            rows = slice(half * HALF, (half + 1) * HALF)
            m = dot_t(branch[rows], wo[...])
            g = gate[rows].astype(F32)
            gate_s = sigmoid(g)
            group = grouped[rows].astype(F32)
            slope = gate_s * (1.0 + g * (1.0 - gate_s))
            grad_gate[rows] = (m * group * slope).astype(BF16)
            e = m * (g * gate_s)
            e = ginv[0, rows] * (
                e
                - jnp.mean(e, axis=1, keepdims=True)
                - group * jnp.mean(e * group, axis=1, keepdims=True)
            )
            kept[rows] = e.astype(BF16)
        moved = (query[...].astype(F32) * arrival[0]).astype(BF16)
        state = t_dot(moved, kept[...])

        @pl.when(head == info[1])
        def _():
            own[...] = state

        @pl.when(head != info[1])
        def _():
            give[...] = state.astype(BF16)

    by_head = lambda h, *_: (0, h)
    cube = lambda h, *_: (h, 0, 0)
    cols = HEADS * VAL
    return call(
        "back_mix",
        body,
        (HEADS,),
        [info],
        [(p,) for p in parts]
        + [
            (wo, (VAL, MODEL), lambda h, *_: (h, 0)),
            (gate, (ROWS, VAL), by_head),
            (grouped, (ROWS, VAL), by_head),
            (ginv, (1, ROWS, 1), cube),
            (query, (ROWS, KEY), by_head),
            (arrival, (1, ROWS, 1), cube),
        ],
        [
            ((ROWS, MODEL), BF16),
            ((ROWS, cols), BF16, (ROWS, VAL), by_head),
            ((ROWS, cols), BF16, (ROWS, VAL), by_head),
            ((KEY, VAL), F32),
            ((KEY, VAL), BF16),
        ],
        tokens,
        keep=(1, 2),
    )


def retain_back(info, kept, value, decay, key, query, weighted, mine, sibling, arrival, cosine, sine, tokens):
    def body(
        info, kept, value, decay, key, query, weighted, mine, sibling, arrival, cosine, sine,
        grad_query, near_key, near_value,
    ):
        head = pl.program_id(0)
        e = kept[...]
        s = (dot_t(e, value[...]) * decay[0]).astype(BF16)
        state = pick(mine, sibling, info, head)
        gq = dot(s, key[...]) + arrival[0] * dot_t(e, state)
        grad_query[...] = rotate(gq, cosine[...], -sine[...]).astype(BF16)
        near_key[...] = t_dot(s, query[...])
        near_value[...] = t_dot(weighted[0], e)

    by_head = lambda h, *_: (0, h)
    cube = lambda h, *_: (h, 0, 0)
    keys, vals = HEADS * KEY, HEADS * VAL
    return call(
        "retain_back",
        body,
        (HEADS,),
        [info],
        [
            (kept, (ROWS, VAL), by_head),
            (value, (ROWS, VAL), by_head),
            (decay, (1, ROWS, ROWS), cube),
            (key, (ROWS, KEY), by_head),
            (query, (ROWS, KEY), by_head),
            (weighted, (1, ROWS, ROWS), cube),
            (mine,),
            (sibling,),
            (arrival, (1, ROWS, 1), cube),
            (cosine,),
            (sine,),
        ],
        [
            ((ROWS, keys), BF16, (ROWS, KEY), by_head),
            ((ROWS, keys), F32, (ROWS, KEY), by_head),
            ((ROWS, vals), F32, (ROWS, VAL), by_head),
        ],
        tokens,
        keep=True,
    )


def key_value_back(info, mine, sibling, key, value, departure, near_key, near_value, cosine, sine, tokens):
    def body(
        info, mine, sibling, key, value, departure, near_key, near_value, cosine, sine,
        grad_key, grad_value,
    ):
        state = pick(mine, sibling, info, pl.program_id(0))
        gk = near_key[...] + departure[0] * dot_t(value[...], state)
        grad_key[...] = rotate(gk, cosine[...], -sine[...]).astype(BF16)
        gv = near_value[...] + departure[0] * dot(key[...], state)
        grad_value[...] = gv.astype(BF16)

    by_head = lambda h, *_: (0, h)
    keys, vals = HEADS * KEY, HEADS * VAL
    return call(
        "key_value_back",
        body,
        (HEADS,),
        [info],
        [
            (mine,),
            (sibling,),
            (key, (ROWS, KEY), by_head),
            (value, (ROWS, VAL), by_head),
            (departure, (1, ROWS, 1), lambda h, *_: (h, 0, 0)),
            (near_key, (ROWS, KEY), by_head),
            (near_value, (ROWS, VAL), by_head),
            (cosine,),
            (sine,),
        ],
        [
            ((ROWS, keys), BF16, (ROWS, KEY), by_head),
            ((ROWS, vals), BF16, (ROWS, VAL), by_head),
        ],
        tokens,
        keep=True,
    )


def turn(name, info, low, tokens=(), keep=False):
    xs = 2

    def body(info, low, own, other, scratch):
        scratch[...] = low[...].T
        for x in range(xs):
            for y in range(SIDE):
                base = (x * SIDE + y) * CORES * 64
                mine = pl.ds(pl.multiple_of(base + info[1] * 64, 64), 64)
                far = pl.ds(pl.multiple_of(base + (1 - info[1]) * 64, 64), 64)
                own[x, y] = scratch[mine, :]
                other[x, y] = scratch[far, :]

    out = ((SIDE, SIDE, 64, ROWS), BF16, (xs, SIDE, 64, ROWS), lambda i, *_: (i, 0, 0, 0))
    own, other = call(
        name,
        body,
        (SIDE // xs,),
        [info],
        [(low, (ROWS, xs * PART), lambda i, *_: (0, i))],
        [out, out],
        tokens,
        [pltpu.VMEM((xs * PART, ROWS), BF16)],
        keep=keep,
    )
    flat = own.reshape(-1, ROWS), other.reshape(-1, ROWS)
    if keep:
        pin(*flat)
    return flat


def cot_pass(info, parts, w2, tokens):
    xs = 2

    def body(info, a, b, c, d, w2, own, other, out, whole_rows, scratch):
        step = pl.program_id(0)

        @pl.when(step == 0)
        def _():
            for k, part in enumerate((a, b, c, d)):
                whole_rows[:, pl.ds(head_col(info, k), PART)] = part[...]

        out[...] = dot_t(whole_rows[...], w2[...]).astype(BF16)
        cols = pl.ds(pl.multiple_of(step * xs * PART, PART), xs * PART)
        scratch[...] = whole_rows[:, cols].T
        for x in range(xs):
            for y in range(SIDE):
                base = (x * SIDE + y) * CORES * 64
                mine = pl.ds(pl.multiple_of(base + info[1] * 64, 64), 64)
                far = pl.ds(pl.multiple_of(base + (1 - info[1]) * 64, 64), 64)
                own[x, y] = scratch[mine, :]
                other[x, y] = scratch[far, :]

    turned = ((SIDE, SIDE, 64, ROWS), BF16, (xs, SIDE, 64, ROWS), lambda i, *_: (i, 0, 0, 0))
    cols = w2.shape[0]
    own, other, out = call(
        "cot_pass",
        body,
        (2,),
        [info],
        [(p,) for p in parts] + [(w2, (cols // 2, MODEL), lambda i, *_: (i, 0))],
        [turned, turned, ((ROWS, cols), BF16, (ROWS, cols // 2), lambda i, *_: (0, i))],
        tokens,
        [pltpu.VMEM((ROWS, MODEL), BF16), pltpu.VMEM((xs * PART, ROWS), BF16)],
    )
    return own.reshape(-1, ROWS), other.reshape(-1, ROWS), out


def widths(groups):
    return [sum(r.shape[1] for r in rights) for _, rights in groups]


def weight_half(name, groups, arrived=None, tokens=()):
    n_left = len(groups)
    rights = [r for _, rs in groups for r in rs]
    counts = [len(rs) for _, rs in groups]
    n = len(rights)
    width = sum(widths(groups))

    def body(*refs):
        lefts, rest = refs[:n_left], refs[n_left : n_left + n]
        out = refs[-1]
        at = 0
        which = 0
        for left, count in zip(lefts, counts):
            for r in rest[which : which + count]:
                cols = slice(at, at + r.shape[1])
                total = dot(left[...], r[...])
                if arrived is not None:
                    total = total + refs[n_left + n][:, cols].astype(F32)
                out[:, cols] = total.astype(BF16)
                at += r.shape[1]
            which += count

    block = lambda i, *_: (i, 0)
    return call(
        name,
        body,
        (2,),
        [],
        [(left, (ROWS, ROWS), block) for left, _ in groups]
        + [(r,) for r in rights]
        + ([(arrived, (ROWS, width), block)] if arrived is not None else []),
        [((2 * ROWS, width), BF16, (ROWS, width), block)],
        tokens,
        keep=True,
    )[0]


PLANE = [
    [seq_index(x, y, c) for x in range(SIDE) for y in range(SIDE)] for c in range(CORES)
]


def axis_groups(along_x):
    if along_x:
        return [
            [seq_index(x, y, c) for x in range(SIDE)] for y in range(SIDE) for c in range(CORES)
        ]
    return [[seq_index(x, y, c) for y in range(SIDE)] for x in range(SIDE) for c in range(CORES)]


def exchange(total, groups):
    blocks = total
    if total.ndim == 2:
        blocks = total.reshape(len(groups[0]), -1, total.shape[-1])
    blocks = lax.all_to_all(blocks, "seq", 0, 0, axis_index_groups=groups, tiled=True)
    pin(blocks)
    return blocks


def weight_mid(name, blocks, gains, tokens=()):
    count, rows, width = blocks.shape
    step = width // 2
    part = rows // SIDE
    gains = jnp.pad(gains, ((0, EXTRA - gains.shape[0]), (0, step - gains.shape[1])))

    def body(blocks, gains, out):
        total = blocks[0].astype(F32)
        for k in range(1, count):
            total = total + blocks[k].astype(F32)
        for y in range(SIDE):
            out[y, :part] = total[y * part : (y + 1) * part].astype(BF16)
            out[y, part:] = gains[...].astype(BF16)

    return call(
        name,
        body,
        (2,),
        [],
        [(blocks, (count, rows, step), lambda i, *_: (0, 0, i)), (gains,)],
        [
            (
                (SIDE, part + EXTRA, width),
                BF16,
                (SIDE, part + EXTRA, step),
                lambda i, *_: (0, 0, i),
            )
        ],
        tokens,
        keep=True,
    )[0]


def weight_sum(name, blocks, parts, tokens=()):
    count, rows, width = blocks.shape
    extra = rows - 64

    def body(blocks, *outs):
        at = 0
        for out, part in zip(outs, parts):
            cols = slice(at, at + part)
            total = blocks[0, :64, cols].astype(F32)
            for k in range(1, count):
                total = total + blocks[k, :64, cols].astype(F32)
            out[...] = total
            at += part
        if extra:
            total = blocks[0, 64:, :PART].astype(F32)
            for k in range(1, count):
                total = total + blocks[k, 64:, :PART].astype(F32)
            outs[-1][...] = total

    return call(
        name,
        body,
        (1,),
        [],
        [(blocks,)],
        [((64, part), F32) for part in parts] + ([((extra, PART), F32)] if extra else []),
        tokens,
    )


def weight_own_y(name, info, left, rights, arrived, tokens=()):
    n = len(rights)
    width = sum(r.shape[1] for r in rights)
    left = left.reshape(SIDE, SIDE, 64, ROWS)
    arrived = arrived.reshape(SIDE, SIDE, 64, width)
    pin(left)

    def body(info, *refs):
        lefts, rights, got, outs = refs[:2], refs[2 : 2 + n], refs[2 + n : 4 + n], refs[4 + n :]
        step = pl.program_id(0)
        for i in range(2):
            at = 0
            for r in rights:
                cols = slice(at, at + r.shape[1])
                total = dot(lefts[i][...].reshape(HALF, ROWS), r[...])
                total = total + got[i][:, :, :, cols].reshape(HALF, r.shape[1]).astype(F32)
                for s in range(2):

                    @pl.when(step == s)
                    def _():
                        out = outs[2 * s + i]
                        out[:, cols] = total.astype(out.dtype)

                at += r.shape[1]

    def block(j):
        def at(i, info):
            return (0, lax.rem(info[Y_AT] + ORDER_OF(2 * i + j), SIDE), 0, 0)

        return at

    return call(
        name,
        body,
        (2,),
        [info],
        [(left, (SIDE, 1, 64, ROWS), block(j)) for j in range(2)]
        + [(r,) for r in rights]
        + [(arrived, (SIDE, 1, 64, width), block(j)) for j in range(2)],
        [((HALF, width), BF16)] * 3 + [((HALF, width), F32)],
        tokens,
    )


def ORDER_OF(i):
    return jnp.where(i == 0, 2, jnp.where(i == 1, 1, jnp.where(i == 2, 3, 0)))


def phase_sum(name, info, where, base, received, tokens=()):
    width = base.shape[1]

    def body(info, base, a, b, c, *refs):
        outs, scratch = refs[:SIDE], refs[SIDE]
        scratch[...] = base[...] + a[...].astype(F32) + b[...].astype(F32) + c[...].astype(F32)
        for i, k in enumerate(ORDER):
            at = pl.multiple_of(lax.rem(info[where] + k, SIDE) * 64, 64)
            outs[i][...] = scratch[pl.ds(at, 64), :].astype(outs[i].dtype)

    return call(
        name,
        body,
        (1,),
        [info],
        [(base,)] + [(r,) for r in received],
        [((64, width), BF16)] * 3 + [((64, width), F32)],
        tokens,
        [pltpu.VMEM((HALF, width), F32)],
    )


def last_sum(name, base, received, parts):
    def body(base, a, b, c, *outs):
        at = 0
        for out in outs:
            cols = slice(at, at + out.shape[1])
            out[...] = base[:, cols] + sum(r[:, cols].astype(F32) for r in (a, b, c))
            at += out.shape[1]

    return call(
        name,
        body,
        (1,),
        [],
        [(base,)] + [(r,) for r in received],
        [((64, w), F32) for w in parts],
    )


def shift_of(along_x):
    return (lambda k: seq_shift(k, 0)) if along_x else (lambda k: seq_shift(0, k))


def send_blocks(blocks, along_x):
    shift = shift_of(along_x)
    return [lax.ppermute(b, "seq", shift(k)) for b, k in zip(blocks, ORDER[:3])]


X_AT, Y_AT = 6, 7


def scan_weights(decay, place, reverse):
    x, y, _ = place
    rel = jnp.arange(SIDE)
    origin = lax.rem(y - rel + SIDE, SIDE)
    target = lax.rem(y + rel, SIDE)
    hops = jnp.arange(1, SIDE)
    if reverse:
        row = origin
        before, counts = SIDE * (SIDE - hops - 1), x + (SIDE - hops) < SIDE
        gap = origin[None, :] - target[:, None]
        carry = SIDE - 1 - target
    else:
        row = SIDE - 1 - origin
        before, counts = SIDE * (hops - 1), x >= hops
        gap = target[:, None] - origin[None, :]
        carry = target
    gap = gap.reshape(-1)
    power = jnp.concatenate([row, before, jnp.maximum(gap - 1, 0), carry]).astype(F32)
    keep = jnp.concatenate([row >= 0, counts, gap > 0, carry >= 0]).astype(F32)
    values = keep * jnp.exp(2.0 * jnp.log(decay) * power)
    return jnp.concatenate([decay[None], values, jnp.zeros((4,), F32)])


W_ROW, W_BEFORE, W_ANSWER, W_CARRY = 1, 5, 8, 24
QUARTER = KEY // SIDE


def state_scan(info, weights, own, give, reverse, tag, fills):
    far = 1 if reverse else 0

    def start_body(info, w, own, got, p2, p1, p3, p0, scratch):
        a, b = own[...], got[...].astype(F32)
        scratch[...] = jnp.where(info[1] == far, w[0] * a + b, a + w[0] * b).astype(BF16)
        for k, out in zip(ORDER, (p2, p1, p3, p0)):
            at = pl.multiple_of(lax.rem(info[Y_AT] + k, SIDE) * QUARTER, QUARTER)
            out[...] = scratch[pl.ds(at, QUARTER), :]

    piece = ((QUARTER, VAL), BF16)
    got = lax.ppermute(give, "seq", SWAP)
    sent = call(
        "scan_start" + tag, start_body, (1,), [info, weights], [(own,), (got,)], [piece] * 4,
        fills[0](), scratch=[pltpu.VMEM((KEY, VAL), BF16)],
    )
    at2, at1, at3 = send_blocks(sent[:3], False)
    pieces = [sent[3], at1, at2, at3]

    def row_body(w, p0, p1, p2, p3, total):
        total[...] = sum(
            w[W_ROW + j] * p[...].astype(F32) for j, p in enumerate((p0, p1, p2, p3))
        ).astype(BF16)

    row = call(
        "scan_row" + tag, row_body, (1,), [weights], [(p,) for p in pieces], [piece],
        fills[1](sent[0]),
    )[0]
    at2, at1, at3 = send_blocks([row] * 3, True)

    def answer_body(w, p0, p1, p2, p3, b1, b2, b3, *outs):
        p = [r[...].astype(F32) for r in (p0, p1, p2, p3)]
        before = sum(w[W_BEFORE + j] * r[...].astype(F32) for j, r in enumerate((b1, b2, b3)))
        for k, out in zip(ORDER, outs):
            total = w[W_CARRY + k] * before
            for j in range(SIDE):
                total = total + w[W_ANSWER + SIDE * k + j] * p[j]
            out[...] = total.astype(BF16)

    answers = call(
        "scan_answer" + tag, answer_body, (1,), [weights],
        [(p,) for p in pieces] + [(at1,), (at2,), (at3,)], [piece] * 4, fills[2](row),
    )
    at2, at1, at3 = send_blocks(answers[:3], False)

    def end_body(info, w, b0, b1, b2, b3, own, got, mine, theirs, scratch):
        for k, b in enumerate((b0, b1, b2, b3)):
            at = pl.multiple_of(lax.rem(info[Y_AT] + SIDE - k, SIDE) * QUARTER, QUARTER)
            scratch[pl.ds(at, QUARTER), :] = b[...].astype(F32)
        chip = scratch[...]
        is_far = info[1] == far
        later = w[0] * chip + jnp.where(is_far, own[...], got[...].astype(F32))
        mine[...] = jnp.where(is_far, chip, later).astype(BF16)
        theirs[...] = jnp.where(is_far, later, chip).astype(BF16)

    state = ((KEY, VAL), BF16)
    mine, theirs = call(
        "scan_end" + tag, end_body, (1,), [info, weights],
        [(answers[3],), (at1,), (at2,), (at3,), (own,), (got,)], [state, state],
        fills[3](answers[0]), scratch=[pltpu.VMEM((KEY, VAL), F32)],
    )
    return mine, lax.ppermute(theirs, "seq", SWAP)


def sum_core_x(values, tokens):
    def body(a, b, out):
        out[...] = a[...] + b[...]

    got = lax.ppermute(values, "seq", SWAP)
    values = call(
        "gain_pair", body, (1,), [], [(values,), (got,)], [(values.shape, F32)], tokens
    )[0]
    return values + sum(lax.ppermute(values, "seq", seq_shift(k, 0)) for k in (1, 2, 3))


def shards(layer_in, gain1, wq, wk, wv, wg, wo, gain2, w1, w2, starts, cotangent):
    seq_rank = lax.axis_index("seq")
    head_rank = lax.axis_index("head")
    x, y, core = (
        seq_rank // (SIDE * CORES),
        (seq_rank // CORES) % SIDE,
        seq_rank % CORES,
    )
    place = (x, y, core)
    PINNED.clear()
    info = jnp.stack(
        [head_rank, core] + [(head_rank + k) % SIDE for k in ORDER] + [x, y]
    ).astype(jnp.int32)
    gain1, gain2 = gain1[None], gain2[None]

    offsets = jnp.arange(ROWS, dtype=jnp.int32)
    positions = seq_rank * ROWS + offsets
    member = positions[:, None] >= starts[None, :]
    doc_ids = jnp.sum(member.astype(jnp.int32), axis=-1) - 1
    last_start = jnp.max(jnp.where(member, starts[None, :], 0), axis=-1)
    relative = (positions - last_start).astype(F32)
    prior_doc = jnp.sum((seq_rank * ROWS - 1 >= starts).astype(jnp.int32)) - 1
    half_dim = KEY // 2
    frequency = jnp.exp(-math.log(10000.0) * jnp.arange(half_dim, dtype=F32) / half_dim)
    angles = relative[:, None] * frequency[None, :]
    cosine, sine = jnp.cos(angles), jnp.sin(angles)
    head_ids = (head_rank * HEADS + jnp.arange(HEADS, dtype=jnp.int32)).astype(F32)
    log_decay = jnp.log1p(-jnp.exp2(-5.0 - head_ids))
    gap_grid = offsets[:, None] - offsets[None, :]
    keep = (gap_grid >= 0) & (doc_ids[:, None] == doc_ids[None, :])
    gap_float = jnp.where(gap_grid >= 0, gap_grid, 0).astype(F32)
    decay = jnp.where(keep[None], jnp.exp(gap_float[None] * log_decay[:, None, None]), 0.0)
    step_float = offsets.astype(F32)
    arrival = jnp.exp((step_float[None, :] + 1.0) * log_decay[:, None]) * (
        doc_ids == prior_doc
    ).astype(F32)
    departure = jnp.exp((ROWS - 1.0 - step_float)[None, :] * log_decay[:, None]) * (
        doc_ids == doc_ids[ROWS - 1]
    ).astype(F32)
    arrival, departure = arrival[:, :, None], departure[:, :, None]
    pin(decay)
    rank_decay = lax.dynamic_index_in_dim(jnp.exp(ROWS * log_decay), core, 0, False)
    ahead = scan_weights(rank_decay, place, False)
    behind = scan_weights(rank_decay, place, True)

    tables = (arrival, departure, ahead, behind, info)
    x_parts = ring_gather(
        layer_in[:HALF], layer_in[HALF:], lambda r, l: relay(r, l, tables)
    )
    low1, mean1, inv1, cot_again, x_rows = norm1(info, x_parts, gain1, cotangent)
    cot_parts = gather_direct(cot_again)
    key, value, own, give = key_value(info, low1, wk, wv, cosine, sine, departure)
    made = {}

    def fill_query():
        made["q"] = query_part(low1, wq, key, value, decay, cosine, sine, (give,))
        return (made["q"][0],)

    def fill_gate(token):
        made["gate"] = matmul_cols("gate", low1, wg, BF16, (token, *cot_parts[1:]))
        return (made["gate"],)

    mine, sibling = state_scan(
        info, ahead, own, give, False, "_a", (fill_query, fill_gate, lambda token: (), lambda token: ())
    )
    query, weighted, within = made["q"]
    gate = made["gate"]
    mixed, grouped, ginv, *blocks = mix(
        info, within, gate, query, mine, sibling, arrival, wo, ()
    )
    pieces, sent = ring_scatter(*blocks[:6])
    cot_own, cot_other, grad_hidden = cot_pass(info, cot_parts, w2, sent)
    low1_own, low1_other = turn("turn_low1", info, low1, (cot_own,), True)
    b_parts = ring_gather(*sum_branch(blocks[6], pieces, (grad_hidden, low1_own)))

    low2, mean2, inv2, middle, hidden, grad_pre = feed_up(
        info, x_rows, b_parts, gain2, w1, grad_hidden, (cot_own,)
    )
    low2_own, low2_other = turn("turn_low2", info, low2)
    feed_other = weight_half(
        "feed_other", [(cot_other, [hidden]), (low2_other, [grad_pre])], None, (low2_own,)
    )
    *blocks, sums = back_blocks(
        "back_feed", info, [(grad_pre, w1)], gain2, low2, (feed_other,)
    )
    pieces, sent = ring_scatter(*blocks[:6])
    feed_got = lax.ppermute(feed_other, "seq", SWAP)
    feed_total = weight_half(
        "feed_own", [(cot_own, [hidden]), (low2_own, [grad_pre])], feed_got
    )
    grad_middle, gain2_grad, half_a, half_b = norm_back(
        "norm_back2", info, blocks[6], sums, pieces, gain2, middle, mean2, inv2, cotangent, True,
        (feed_total,),
    )
    g_parts = ring_gather(half_a, half_b)
    feed_blocks = exchange(feed_total, PLANE)

    branch, grad_gate, kept, own, give = back_mix(
        info, g_parts, wo, gate, grouped, ginv, query, arrival, (feed_total,)
    )

    branch_own, branch_other = turn("turn_branch", info, branch, (give,), True)
    grad_query, near_key, near_value = retain_back(
        info, kept, value, decay, key, query, weighted, mine, sibling, arrival, cosine, sine,
        (branch_own,),
    )
    mix_other = weight_half(
        "mix_other",
        [(branch_other, [mixed]), (low1_other, [grad_gate, grad_query])],
        None,
        (grad_query,),
    )
    mix_got = lax.ppermute(mix_other, "seq", SWAP)

    def fill_own(token):
        made["own"] = weight_half(
            "mix_own",
            [(branch_own, [mixed]), (low1_own, [grad_gate, grad_query])],
            mix_got,
            (token,),
        )
        return (made["own"],)

    feed = matmul_cols("feed_down", hidden, w2, BF16, (mix_other,), 1024)
    fed = lax.psum_scatter(feed, "head", scatter_dimension=1, tiled=True)

    far_mine, far_sibling = state_scan(
        info, behind, own, give, True, "_b",
        (lambda: (feed, feed_blocks), fill_own, lambda token: (), lambda token: (fed,)),
    )
    mix_x = exchange(gated(made["own"], (far_mine,)), axis_groups(True))
    grad_key, grad_value = key_value_back(
        info, far_mine, far_sibling, key, value, departure, near_key, near_value, cosine, sine,
        (),
    )
    kv_other = weight_half(
        "kv_other", [(low1_other, [grad_key, grad_value])]
    )
    kv_got = lax.ppermute(kv_other, "seq", SWAP)
    *blocks, sums = back_blocks(
        "back_proj", info,
        [(grad_query, wq), (grad_gate, wg), (grad_key, wk), (grad_value, wv)],
        gain1, low1, (kv_other, feed_blocks),
    )
    pieces, sent = ring_scatter(*blocks[:6])
    kv_blocks = weight_own_y(
        "kv_own", info, low1_own, [grad_key, grad_value], kv_got, sent
    )

    grad_x, gain1_grad = norm_back(
        "norm_back1", info, blocks[6], sums, pieces, gain1, layer_in, mean1, inv1, grad_middle,
        False, (kv_blocks[0],),
    )
    keys, vals = HEADS * KEY, HEADS * VAL
    kv_sent = send_blocks(kv_blocks[:3], False)
    kv_half = phase_sum("kv_mid", info, X_AT, kv_blocks[3], kv_sent)
    gains = sum_core_x(jnp.concatenate([gain1_grad, gain2_grad], axis=0), (mix_x,))
    mix_half = weight_mid("mix_mid", mix_x, gains)
    grad_w2, grad_w1 = weight_sum("feed_sum", feed_blocks, [vals, vals], (mix_half,))
    grad_wo, grad_wg, grad_wq, gains = weight_sum(
        "mix_sum", exchange(mix_half, axis_groups(False)), [vals, vals, keys]
    )
    grad_wk, grad_wv = last_sum(
        "kv_sum", kv_half[3], send_blocks(kv_half[:3], True), (keys, vals)
    )
    output = (middle + fed.astype(F32)).astype(BF16)
    return (
        output,
        grad_x,
        gains[0],
        grad_wq,
        grad_wk,
        grad_wv,
        grad_wg,
        grad_wo.T,
        gains[1],
        grad_w1,
        grad_w2.T,
    )


def solution(mesh):
    rows = P("seq", "head")
    cols = P(None, "head")
    tall = P("head", None)
    return jax.shard_map(
        shards,
        mesh=mesh,
        in_specs=(rows, P(), cols, cols, cols, cols, tall, P(), cols, tall, P(), rows),
        out_specs=(
            rows, rows, P("head"), rows, rows, rows, rows, P("head", "seq"), P("head"), rows,
            P("head", "seq"),
        ),
        check_vma=False,
    )
```

profile of v0, /device:TPU:0, one launch (start us, length us, event | category | flops | bytes accessed | tf_op | source)
XLA Modules:
  0.0 385.8 jit_solution(18253414669047994412)
XLA Ops:
  28.8 4.4 %collective-permute-done.3.refs_5_ = bf16[256,512]{1,0:T(8,128)(2,1)S(1)} collective-permute-done((bf16[256,512]{1,0:T(8,128)(2,1)S(1)}, bf16[256,512]{1,0:T(8,128)(2,1)S(1)}, u32[]{:S(2)}, u32[]{:S(2)}) %collective-permute-start.3) | collective-permute-done | bytes 262176 | tf_op jit(solution)/shard_map/ppermute | solution.py:48
  36.8 4.4 %collective-permute-start.8 = (bf16[512,512]{1,0:T(8,128)(2,1)S(1)}, bf16[512,512]{1,0:T(8,128)(2,1)S(1)}, u32[]{:S(2)}, u32[]{:S(2)}) collective-permute-start(bf16[512,512]{1,0:T(8,128)(2,1)S(1)} %get-tuple-element.131.refs_1_), channel_id=1, source_target_pairs={{0,2},{1,3},{2,0},{3,1},{4,6},{5,7},{6,4},{7,5},{8,10},{9,11},{10,... | collective-permute-start | bytes 1572872 | tf_op jit(solution)/shard_map/ppermute | solution.py:95
  41.3 6.2 %key_value.1 = (bf16[512,512]{1,0:T(8,128)(2,1)}, bf16[512,1024]{1,0:T(8,128)(2,1)}, f32[256,512]{1,0:T(8,128)S(1)}, bf16[256,512]{1,0:T(8,128)(2,1)S(1)}) custom-call(s32[8]{0:T(128)S(1)} %stack.35.refs_6_.refs_0_, bf16[512,2048]{1,0:T(8,128)(2,1)S(1)} %get-tuple-element.123.refs_1_.refs_0_.refs_15_.refs_16_, bf16[2048,512]{1,0:T(8,128)(2,1)S(1)} %copy-done.8, ...), custom_call_target="tpu_custom_call" | custom-call | flops 8800000000 | tf_op jit(solution)/shard_map/key_value/pallas_call | solution.py:192
  47.5 6.0 %query_part.1 = (bf16[512,512]{1,0:T(8,128)(2,1)}, bf16[2,512,512]{2,1,0:T(8,128)(2,1)}, f32[512,1024]{1,0:T(8,128)S(1)}) custom-call(bf16[512,2048]{1,0:T(8,128)(2,1)S(1)} %get-tuple-element.123.refs_1_.refs_0_.refs_15_.refs_16_, bf16[2048,512]{1,0:T(8,128)(2,1)S(1)} %copy-done.6, bf16[512,512]{1,0:T(8,128)(2,1)} %get-tuple-element.124.refs_2_.refs_4_.refs_3_, ...), custom_call_target="tpu_custom_call" | custom-call | flops 6600000000 | tf_op jit(solution)/shard_map/query_part/pallas_call | solution.py:192
  87.3 6.7 %mix.1 = (bf16[512,1024]{1,0:T(8,128)(2,1)}, bf16[512,1024]{1,0:T(8,128)(2,1)}, f32[2,512,1]{2,1,0:T(8,128)S(1)}, bf16[256,512]{1,0:T(8,128)(2,1)S(1)}, bf16[256...) custom-call(s32[8]{0:T(128)S(1)} %stack.35.refs_6_.refs_0_, ...), custom_call_target="tpu_custom_call" | custom-call | flops 9900000256 | tf_op jit(solution)/shard_map/mix/pallas_call | solution.py:192
  118.3 8.6 %collective-permute-start.27 = (bf16[256,512]{1,0:T(8,128)(2,1)S(1)}, bf16[256,512]{1,0:T(8,128)(2,1)S(1)}, u32[]{:S(2)}, u32[]{:S(2)}) collective-permute-start(bf16[256,512]{1,0:T(8,128)(2,1)S(1)} %get-tuple-element.152.refs_3_), channel_id=1, source_target_pairs={{0,1},{1,2},{2,3},{3,0},{4,5},{5,6},{6,7},{7,4},{8,9},{9,10},{10,1... | collective-permute-start | bytes 786440 | tf_op jit(solution)/shard_map/ppermute | solution.py:48
  133.4 4.0 %collective-permute-done.27.refs_5_ = bf16[256,512]{1,0:T(8,128)(2,1)S(1)} collective-permute-done((bf16[256,512]{1,0:T(8,128)(2,1)S(1)}, bf16[256,512]{1,0:T(8,128)(2,1)S(1)}, u32[]{:S(2)}, u32[]{:S(2)}) %collective-permute-start.27) | collective-permute-done | bytes 262176 | tf_op jit(solution)/shard_map/ppermute | solution.py:48
  140.7 7.4 %feed_up.1 = (bf16[512,2048]{1,0:T(8,128)(2,1)S(1)}, f32[512,1]{1,0:T(8,128)}, f32[512,1]{1,0:T(8,128)}, f32[512,512]{1,0:T(8,128)}, bf16[512,1024]{1,0:T(8,128)(2,1)S(1)}, /*index=5*/bf16[512,1024]{1,0:T(8,128)(2,1)S(1)}) custom-call(s32[8]{0:T(128)S(1)} %stack.35.refs_6_.refs_0_, bf16[4,512,512]{2,1,0:T(8,128)(2,1)} %get-tuple-element.122.refs_1_, ...), custom_call_target="tpu_custom_call" | custom-call | flops 12099999744 | tf_op jit(solution)/shard_map/feed_up/pallas_call | solution.py:192
  149.7 3.9 %feed_other.1.refs_8_ = bf16[1024,2048]{1,0:T(8,128)(2,1)} custom-call(bf16[1024,512]{1,0:T(8,128)(2,1)S(1)} %bitcast.40, bf16[1024,512]{1,0:T(8,128)(2,1)S(1)} %bitcast.43, bf16[512,1024]{1,0:T(8,128)(2,1)S(1)} %get-tuple-element.154.refs_2_.refs_0_, bf16[512,1024]{1,0:T(8,128)(2,1)S(1)} %get-tuple-element.155.refs_3_.refs_1_, bf16[1024,512]{1,0:T(8,128)(2,1)S(1)} %bitcast.41), custom_call_target="tpu_custom_call" | custom-call | flops 5500000256 | tf_op jit(solution)/shard_map/feed_other/pallas_call | solution.py:192
  153.6 5.6 %back_feed.1 = (bf16[272,512]{1,0:T(8,128)(2,1)S(1)}, bf16[256,512]{1,0:T(8,128)(2,1)S(1)}, bf16[272,512]{1,0:T(8,128)(2,1)S(1)}, bf16[256,512]{1,0:T(8,128)(2,1...) custom-call(s32[8]{0:T(128)S(1)} %stack.35.refs_6_.refs_0_, ...), custom_call_target="tpu_custom_call" | custom-call | flops 7699999744 | tf_op jit(solution)/shard_map/back_feed/pallas_call | solution.py:192
  177.9 6.2 %all-to-all-start = ((bf16[16,64,2048]{2,1,0:T(8,128)(2,1)}), bf16[16,64,2048]{2,1,0:T(8,128)(2,1)}, u32[]{:S(2)}, u32[]{:S(2)}) async-start(bf16[16,64,2048]{2,1,0:T(8,128)(2,1)} %bitcast.47), calls=%async_computation.1 | async-start | bytes 8388608 | tf_op jit(solution)/shard_map/all_to_all | solution.py:897
  184.3 4.3 %norm_back2.1 = (f32[512,512]{1,0:T(8,128)}, f32[1,512]{1,0:T(1,128)S(1)}, bf16[256,512]{1,0:T(8,128)(2,1)S(1)}, bf16[256,512]{1,0:T(8,128)(2,1)S(1)}) custom-call(s32[8]{0:T(128)S(1)} %stack.35.refs_6_.refs_0_, f32[512,512]{1,0:T(8,128)} %get-tuple-element.160.refs_1_, f32[16,512]{1,0:T(8,128)S(1)} %get-tuple-element.161.refs_2_, ...), custom_call_target="tpu_custom_call" | custom-call | flops 109999996928 | tf_op jit(solution)/shard_map/norm_back2/pallas_call | solution.py:192
  208.1 7.0 %back_mix.1 = (bf16[512,2048]{1,0:T(8,128)(2,1)S(1)}, bf16[512,1024]{1,0:T(8,128)(2,1)}, bf16[512,1024]{1,0:T(8,128)(2,1)}, f32[256,512]{1,0:T(8,128)S(1)}, bf16[256,512]{1,0:T(8,128)(2,1)S(1)}) custom-call(s32[8]{0:T(128)S(1)} %stack.35.refs_6_.refs_0_, bf16[256,512]{1,0:T(8,128)(2,1)S(1)} %get-tuple-element.170.refs_1_, ...), custom_call_target="tpu_custom_call" | custom-call | flops 6600000000 | tf_op jit(solution)/shard_map/back_mix/pallas_call | solution.py:192
  217.7 5.9 %retain_back.1 = (bf16[512,512]{1,0:T(8,128)(2,1)}, f32[512,512]{1,0:T(8,128)}, f32[512,1024]{1,0:T(8,128)}) custom-call(s32[8]{0:T(128)S(1)} %stack.35.refs_6_.refs_0_, bf16[512,1024]{1,0:T(8,128)(2,1)} %get-tuple-element.180.refs_1_, bf16[512,1024]{1,0:T(8,128)(2,1)} %get-tuple-element.125.refs_3_.refs_2_.refs_4_, ...), custom_call_target="tpu_custom_call" | custom-call | flops 660000000 | tf_op jit(solution)/shard_map/retain_back/pallas_call | solution.py:192
  223.6 6.8 %mix_other.1.refs_2_ = bf16[1024,2560]{1,0:T(8,128)(2,1)} custom-call(bf16[1024,512]{1,0:T(8,128)(2,1)} %bitcast.52, bf16[1024,512]{1,0:T(8,128)(2,1)} %bitcast.48, bf16[512,1024]{1,0:T(8,128)(2,1)} %get-tuple-element.178.refs_2_, bf16[512,1024]{1,0:T(8,128)(2,1)} %get-tuple-element.179.refs_3_.refs_2_, ...), custom_call_target="tpu_custom_call" | custom-call | flops 198000000 | tf_op jit(solution)/shard_map/mix_other/pallas_call | solution.py:192
  244.6 7.7 %mix_own.1.refs_5_.refs_0_ = bf16[1024,2560]{1,0:T(8,128)(2,1)} custom-call(bf16[1024,512]{1,0:T(8,128)(2,1)} %bitcast.51, bf16[1024,512]{1,0:T(8,128)(2,1)} %bitcast.46, bf16[512,1024]{1,0:T(8,128)(2,1)} %get-tuple-element.178.refs_2_, bf16[512,1024]{1,0:T(8,128)(2,1)} %get-tuple-element.179.refs_3_.refs_2_, ...), custom_call_target="tpu_custom_call" | custom-call | flops 1100000000 | tf_op jit(solution)/shard_map/mix_own/pallas_call | solution.py:192
  272.2 5.2 %all-to-all-start.1 = ((bf16[4,256,2560]{2,1,0:T(8,128)(2,1)}), bf16[4,256,2560]{2,1,0:T(8,128)(2,1)}, u32[]{:S(2)}, u32[]{:S(2)}) async-start(bf16[4,256,2560]{2,1,0:T(8,128)(2,1)} %bitcast.44), calls=%async_computation.2 | async-start | bytes 10485760 | tf_op jit(solution)/shard_map/all_to_all | solution.py:897
  277.5 4.6 %key_value_back.1 = (bf16[512,512]{1,0:T(8,128)(2,1)}, bf16[512,1024]{1,0:T(8,128)(2,1)}) custom-call(s32[8]{0:T(128)S(1)} %stack.35.refs_6_.refs_0_, bf16[256,512]{1,0:T(8,128)(2,1)S(1)} %copy-done.30, bf16[256,512]{1,0:T(8,128)(2,1)S(1)} %collective-permute-done.56.refs_2_, bf16[512,512]{1,0:T(8,128)(2,1)} %get-tuple-element.124.refs_2_.refs_4_.refs_3_, ...), custom_call_target="tpu_custom_call" | custom-call | flops 109999996928 | tf_op jit(solution)/shard_map/key_value_back/pallas_call | solution.py:192
  282.1 5.1 %kv_other.1.refs_17_ = bf16[1024,1536]{1,0:T(8,128)(2,1)} custom-call(bf16[1024,512]{1,0:T(8,128)(2,1)} %bitcast.49, bf16[512,512]{1,0:T(8,128)(2,1)} %get-tuple-element.197.refs_1_.refs_3_, bf16[512,1024]{1,0:T(8,128)(2,1)} %get-tuple-element.198.refs_2_.refs_4_), custom_call_target="tpu_custom_call" | custom-call | flops 990000000 | tf_op jit(solution)/shard_map/kv_other/pallas_call | solution.py:192
  287.7 11.6 %back_proj.1 = (bf16[272,512]{1,0:T(8,128)(2,1)S(1)}, bf16[256,512]{1,0:T(8,128)(2,1)S(1)}, bf16[272,512]{1,0:T(8,128)(2,1)S(1)}, bf16[256,512]{1,0:T(8,128)(2,1...) custom-call(s32[8]{0:T(128)S(1)} %stack.35.refs_6_.refs_0_, ...), custom_call_target="tpu_custom_call" | custom-call | flops 110000000 | tf_op jit(solution)/shard_map/back_proj/pallas_call | solution.py:192
  311.6 6.7 %kv_own.1 = (bf16[256,1536]{1,0:T(8,128)(2,1)S(1)}, bf16[256,1536]{1,0:T(8,128)(2,1)}, bf16[256,1536]{1,0:T(8,128)(2,1)}, f32[256,1536]{1,0:T(8,128)S(1)}) custom-call(s32[8]{0:T(128)S(1)} %stack.35.refs_6_.refs_0_, bf16[4,4,64,512]{3,2,1,0:T(8,128)(2,1)} %get-tuple-element.150.refs_1_.refs_2_, bf16[4,4,64,512]{3,2,1,0:T(8,128)(2,1)} %get-tuple-element.150.refs_1_.refs_2_, ...), custom_call_target="tpu_custom_call" | custom-call | flops 110000000 | tf_op jit(solution)/shard_map/kv_own/pallas_call | solution.py:192
  327.1 3.9 %collective-permute-done.62.refs_6_ = bf16[256,512]{1,0:T(8,128)(2,1)S(1)} collective-permute-done((bf16[256,512]{1,0:T(8,128)(2,1)S(1)}, bf16[256,512]{1,0:T(8,128)(2,1)S(1)}, u32[]{:S(2)}, u32[]{:S(2)}) %collective-permute-start.62) | collective-permute-done | bytes 262176 | tf_op jit(solution)/shard_map/ppermute | solution.py:52
  351.5 4.4 %all-to-all-start.2 = ((bf16[4,80,2560]{2,1,0:T(8,128)(2,1)}), bf16[4,80,2560]{2,1,0:T(8,128)(2,1)}, u32[]{:S(2)}, u32[]{:S(2)}) async-start(bf16[4,80,2560]{2,1,0:T(8,128)(2,1)} %mix_mid.1.refs_1_), calls=%async_computation.3 | async-start | bytes 3276800 | tf_op jit(solution)/shard_map/all_to_all | solution.py:897
  371.2 4.7 %all-to-all-done.2.refs_0_ = bf16[4,80,2560]{2,1,0:T(8,128)(2,1)} async-done(((bf16[4,80,2560]{2,1,0:T(8,128)(2,1)}), bf16[4,80,2560]{2,1,0:T(8,128)(2,1)}, u32[]{:S(2)}, u32[]{:S(2)}) %all-to-all-start.2) | async-done | bytes 1638432 | tf_op jit(solution)/shard_map/all_to_all | solution.py:897
  (310 shorter events, 228.0 us)
Async XLA Ops:
  8.3 20.5 %collective-permute-start.1 = (bf16[256,512]{1,0:T(8,128)(2,1)S(1)}, bf16[256,512]{1,0:T(8,128)(2,1)S(1)}, u32[]{:S(2)}, u32[]{:S(2)}) collective-permute-start(bf16[256,512]{1,0:T(8,128)(2,1)S(1)} %get-tuple-element.231.refs_2_), channel_id=1, source_target_pairs={{0,1},{1,2},{2,3},{3,0},{4,5},{5,6},{6,7},{7,4},{8,9},{9,10},{10,1... | collective-permute-start | bytes 786440 | tf_op jit(solution)/shard_map/ppermute | solution.py:48
  12.5 16.2 %collective-permute-start.5 = (bf16[256,512]{1,0:T(8,128)(2,1)S(1)}, bf16[256,512]{1,0:T(8,128)(2,1)S(1)}, u32[]{:S(2)}, u32[]{:S(2)}) collective-permute-start(bf16[256,512]{1,0:T(8,128)(2,1)S(1)} %get-tuple-element.232.refs_1_), channel_id=1, source_target_pairs={{0,3},{1,0},{2,1},{3,2},{4,7},{5,4},{6,5},{7,6},{8,11},{9,8},{10,9... | collective-permute-start | bytes 786440 | tf_op jit(solution)/shard_map/ppermute | solution.py:52
  36.8 22.0 %collective-permute-start.7 = (bf16[512,512]{1,0:T(8,128)(2,1)S(1)}, bf16[512,512]{1,0:T(8,128)(2,1)S(1)}, u32[]{:S(2)}, u32[]{:S(2)}) collective-permute-start(bf16[512,512]{1,0:T(8,128)(2,1)S(1)} %get-tuple-element.131.refs_1_), channel_id=1, source_target_pairs={{0,1},{1,2},{2,3},{3,0},{4,5},{5,6},{6,7},{7,4},{8,9},{9,10},{10,1... | collective-permute-start | bytes 1572872 | tf_op jit(solution)/shard_map/ppermute | solution.py:95
  36.8 25.5 %collective-permute-start.8 = (bf16[512,512]{1,0:T(8,128)(2,1)S(1)}, bf16[512,512]{1,0:T(8,128)(2,1)S(1)}, u32[]{:S(2)}, u32[]{:S(2)}) collective-permute-start(bf16[512,512]{1,0:T(8,128)(2,1)S(1)} %get-tuple-element.131.refs_1_), channel_id=1, source_target_pairs={{0,2},{1,3},{2,0},{3,1},{4,6},{5,7},{6,4},{7,5},{8,10},{9,11},{10,... | collective-permute-start | bytes 1572872 | tf_op jit(solution)/shard_map/ppermute | solution.py:95
  41.2 21.1 %collective-permute-start.9 = (bf16[512,512]{1,0:T(8,128)(2,1)S(1)}, bf16[512,512]{1,0:T(8,128)(2,1)S(1)}, u32[]{:S(2)}, u32[]{:S(2)}) collective-permute-start(bf16[512,512]{1,0:T(8,128)(2,1)S(1)} %get-tuple-element.131.refs_1_), channel_id=1, source_target_pairs={{0,3},{1,0},{2,1},{3,2},{4,7},{5,4},{6,5},{7,6},{8,11},{9,8},{10,9... | collective-permute-start | bytes 1572872 | tf_op jit(solution)/shard_map/ppermute | solution.py:95
  97.3 16.6 %collective-permute-start.22 = (bf16[256,512]{1,0:T(8,128)(2,1)S(1)}, bf16[256,512]{1,0:T(8,128)(2,1)S(1)}, u32[]{:S(2)}, u32[]{:S(2)}) collective-permute-start(bf16[256,512]{1,0:T(8,128)(2,1)S(1)} %get-tuple-element.144), channel_id=1, source_target_pairs={{0,1},{1,2},{2,3},{3,0},{4,5},{5,6},{6,7},{7,4},{8,9},{9,10},{10,1... | collective-permute-start | bytes 786440 | tf_op jit(solution)/shard_map/ppermute | solution.py:48
  97.3 16.6 %collective-permute-start.23 = (bf16[256,512]{1,0:T(8,128)(2,1)S(1)}, bf16[256,512]{1,0:T(8,128)(2,1)S(1)}, u32[]{:S(2)}, u32[]{:S(2)}) collective-permute-start(bf16[256,512]{1,0:T(8,128)(2,1)S(1)} %get-tuple-element.145), channel_id=1, source_target_pairs={{0,3},{1,0},{2,1},{3,2},{4,7},{5,4},{6,5},{7,6},{8,11},{9,8},{10,9... | collective-permute-start | bytes 786440 | tf_op jit(solution)/shard_map/ppermute | solution.py:52
  115.0 15.1 %collective-permute-start.26 = (bf16[256,512]{1,0:T(8,128)(2,1)S(1)}, bf16[256,512]{1,0:T(8,128)(2,1)S(1)}, u32[]{:S(2)}, u32[]{:S(2)}) collective-permute-start(bf16[256,512]{1,0:T(8,128)(2,1)S(1)} %get-tuple-element.151.refs_2_), channel_id=1, source_target_pairs={{0,1},{1,2},{2,3},{3,0},{4,5},{5,6},{6,7},{7,4},{8,9},{9,10},{10,1... | collective-permute-start | bytes 786440 | tf_op jit(solution)/shard_map/ppermute | solution.py:48
  118.3 19.1 %collective-permute-start.27 = (bf16[256,512]{1,0:T(8,128)(2,1)S(1)}, bf16[256,512]{1,0:T(8,128)(2,1)S(1)}, u32[]{:S(2)}, u32[]{:S(2)}) collective-permute-start(bf16[256,512]{1,0:T(8,128)(2,1)S(1)} %get-tuple-element.152.refs_3_), channel_id=1, source_target_pairs={{0,1},{1,2},{2,3},{3,0},{4,5},{5,6},{6,7},{7,4},{8,9},{9,10},{10,1... | collective-permute-start | bytes 786440 | tf_op jit(solution)/shard_map/ppermute | solution.py:48
  153.6 20.4 %collective-permute-start.38 = (bf16[1024,2048]{1,0:T(8,128)(2,1)}, bf16[1024,2048]{1,0:T(8,128)(2,1)S(1)}, u32[]{:S(2)}, u32[]{:S(2)}) collective-permute-start(bf16[1024,2048]{1,0:T(8,128)(2,1)} %feed_other.1.refs_8_), channel_id=1, source_target_pairs={{0,4},{4,0},{8,12},{12,8},{16,20},{20,16},{24,28},{28,24},{32,36},... | collective-permute-start | bytes 12582920 | tf_op jit(solution)/shard_map/ppermute | solution.py:1253
  162.2 22.0 %collective-permute-start.34 = (bf16[256,512]{1,0:T(8,128)(2,1)S(1)}, bf16[256,512]{1,0:T(8,128)(2,1)S(1)}, u32[]{:S(2)}, u32[]{:S(2)}) collective-permute-start(bf16[256,512]{1,0:T(8,128)(2,1)S(1)} %get-tuple-element.164), channel_id=1, source_target_pairs={{0,1},{1,2},{2,3},{3,0},{4,5},{5,6},{6,7},{7,4},{8,9},{9,10},{10,1... | collective-permute-start | bytes 786440 | tf_op jit(solution)/shard_map/ppermute | solution.py:48
  162.2 22.0 %collective-permute-start.35 = (bf16[272,512]{1,0:T(8,128)(2,1)S(1)}, bf16[272,512]{1,0:T(8,128)(2,1)S(1)}, u32[]{:S(2)}, u32[]{:S(2)}) collective-permute-start(bf16[272,512]{1,0:T(8,128)(2,1)S(1)} %get-tuple-element.165), channel_id=1, source_target_pairs={{0,3},{1,0},{2,1},{3,2},{4,7},{5,4},{6,5},{7,6},{8,11},{9,8},{10,9... | collective-permute-start | bytes 835592 | tf_op jit(solution)/shard_map/ppermute | solution.py:52
  169.6 14.6 %collective-permute-start.37 = (bf16[256,512]{1,0:T(8,128)(2,1)}, bf16[256,512]{1,0:T(8,128)(2,1)}, u32[]{:S(2)}, u32[]{:S(2)}) collective-permute-start(bf16[256,512]{1,0:T(8,128)(2,1)} %add_convert_fusion.4), channel_id=1, source_target_pairs={{0,3},{1,0},{2,1},{3,2},{4,7},{5,4},{6,5},{7,6},{8,11},{9,8},{10,9... | collective-permute-start | bytes 786440 | tf_op jit(solution)/shard_map/ppermute | solution.py:52
  177.9 60.7 %all-to-all-start = ((bf16[16,64,2048]{2,1,0:T(8,128)(2,1)}), bf16[16,64,2048]{2,1,0:T(8,128)(2,1)}, u32[]{:S(2)}, u32[]{:S(2)}) async-start(bf16[16,64,2048]{2,1,0:T(8,128)(2,1)} %bitcast.47), calls=%async_computation.1 | async-start | bytes 8388608 | tf_op jit(solution)/shard_map/all_to_all | solution.py:897
  184.2 82.5 %reduce-scatter.2.cloned.1.call-start = ((), (), s32[]{:S(2)}) async-start(), calls=%async_computation.4 | async-start | bytes 2621440 | tf_op jit(solution)/shard_map/reduce_scatter | solution.py:1291
  215.1 19.6 %collective-permute-start.45 = (bf16[256,512]{1,0:T(8,128)(2,1)S(1)}, bf16[256,512]{1,0:T(8,128)(2,1)S(1)}, u32[]{:S(2)}, u32[]{:S(2)}) collective-permute-start(bf16[256,512]{1,0:T(8,128)(2,1)S(1)} %get-tuple-element.175.refs_2_), channel_id=1, source_target_pairs={{0,4},{4,0},{8,12},{12,8},{16,20},{20,16},{24,28},{28,24},{32,36},... | collective-permute-start | bytes 786440 | tf_op jit(solution)/shard_map/ppermute | solution.py:1103
  272.2 66.6 %all-to-all-start.1 = ((bf16[4,256,2560]{2,1,0:T(8,128)(2,1)}), bf16[4,256,2560]{2,1,0:T(8,128)(2,1)}, u32[]{:S(2)}, u32[]{:S(2)}) async-start(bf16[4,256,2560]{2,1,0:T(8,128)(2,1)} %bitcast.44), calls=%async_computation.2 | async-start | bytes 10485760 | tf_op jit(solution)/shard_map/all_to_all | solution.py:897
  287.2 24.4 %collective-permute-start.63 = (bf16[1024,1536]{1,0:T(8,128)(2,1)}, bf16[1024,1536]{1,0:T(8,128)(2,1)S(1)}, u32[]{:S(2)}, u32[]{:S(2)}) collective-permute-start(bf16[1024,1536]{1,0:T(8,128)(2,1)} %kv_other.1.refs_17_), channel_id=1, source_target_pairs={{0,4},{4,0},{8,12},{12,8},{16,20},{20,16},{24,28},{28,24},{32,36},... | collective-permute-start | bytes 9437192 | tf_op jit(solution)/shard_map/ppermute | solution.py:1305
  301.8 22.1 %collective-permute-start.59 = (bf16[256,512]{1,0:T(8,128)(2,1)S(1)}, bf16[256,512]{1,0:T(8,128)(2,1)S(1)}, u32[]{:S(2)}, u32[]{:S(2)}) collective-permute-start(bf16[256,512]{1,0:T(8,128)(2,1)S(1)} %get-tuple-element.203), channel_id=1, source_target_pairs={{0,1},{1,2},{2,3},{3,0},{4,5},{5,6},{6,7},{7,4},{8,9},{9,10},{10,1... | collective-permute-start | bytes 786440 | tf_op jit(solution)/shard_map/ppermute | solution.py:48
  303.8 20.1 %collective-permute-start.60 = (bf16[272,512]{1,0:T(8,128)(2,1)S(1)}, bf16[272,512]{1,0:T(8,128)(2,1)S(1)}, u32[]{:S(2)}, u32[]{:S(2)}) collective-permute-start(bf16[272,512]{1,0:T(8,128)(2,1)S(1)} %get-tuple-element.204), channel_id=1, source_target_pairs={{0,3},{1,0},{2,1},{3,2},{4,7},{5,4},{6,5},{7,6},{8,11},{9,8},{10,9... | collective-permute-start | bytes 835592 | tf_op jit(solution)/shard_map/ppermute | solution.py:52
  318.4 37.5 %collective-permute-start.68 = (bf16[256,1536]{1,0:T(8,128)(2,1)S(1)}, bf16[256,1536]{1,0:T(8,128)(2,1)}, u32[]{:S(2)}, u32[]{:S(2)}) collective-permute-start(bf16[256,1536]{1,0:T(8,128)(2,1)S(1)} %get-tuple-element.210.refs_12_), channel_id=1, source_target_pairs={{0,16},{4,20},{8,24},{12,28},{16,0},{20,4},{24,8},{28,12},{32,48},... | collective-permute-start | bytes 2359304 | tf_op jit(solution)/shard_map/ppermute | solution.py:1059
  320.6 35.3 %collective-permute-start.69 = (bf16[256,1536]{1,0:T(8,128)(2,1)}, bf16[256,1536]{1,0:T(8,128)(2,1)}, u32[]{:S(2)}, u32[]{:S(2)}) collective-permute-start(bf16[256,1536]{1,0:T(8,128)(2,1)} %get-tuple-element.217), channel_id=1, source_target_pairs={{0,8},{4,12},{8,16},{12,20},{16,24},{20,28},{24,0},{28,4},{32,40},... | collective-permute-start | bytes 2359304 | tf_op jit(solution)/shard_map/ppermute | solution.py:1059
  322.3 33.6 %collective-permute-start.70 = (bf16[256,1536]{1,0:T(8,128)(2,1)}, bf16[256,1536]{1,0:T(8,128)(2,1)}, u32[]{:S(2)}, u32[]{:S(2)}) collective-permute-start(bf16[256,1536]{1,0:T(8,128)(2,1)} %get-tuple-element.218), channel_id=1, source_target_pairs={{0,24},{4,28},{8,0},{12,4},{16,8},{20,12},{24,16},{28,20},{32,56},... | collective-permute-start | bytes 2359304 | tf_op jit(solution)/shard_map/ppermute | solution.py:1059
  351.5 24.3 %all-to-all-start.2 = ((bf16[4,80,2560]{2,1,0:T(8,128)(2,1)}), bf16[4,80,2560]{2,1,0:T(8,128)(2,1)}, u32[]{:S(2)}, u32[]{:S(2)}) async-start(bf16[4,80,2560]{2,1,0:T(8,128)(2,1)} %mix_mid.1.refs_1_), calls=%async_computation.3 | async-start | bytes 3276800 | tf_op jit(solution)/shard_map/all_to_all | solution.py:897
  (99 other events, 1059.8 us)
Sparse Core Ops, SparseCore 0:
  234.9 31.0 reduce-scatter.1
where the time goes:
time: 392 us; the launch traced here: 386 us
  Pallas kernels  144 us (37%)
  starting transfers between devices  138 us (35%)
  waiting for transfers between devices  73.9 us (19%)
  between operations  16.5 us (4%)
  other arithmetic  8.81 us (2%)
  local copies, waits for them, and re-layouts  5.19 us (1%)
    pallas_call x40, Pallas kernels, call(): pl.pallas_call(run, name=name, grid_spec=pltpu.PrefetchScalarGridSpec(num...  144 us
    ppermute x18, starting transfers between devices, down(): return lax.ppermute(block, 'head', head_shift(SIDE - 1))  53 us
    ppermute x24, starting transfers between devices, send_blocks(): return [lax.ppermute(b, 'seq', shift(k)) for b, k in zip(blocks, ORDER[:3])]  45 us
    ppermute x18, waiting for transfers between devices, up(): return lax.ppermute(block, 'head', head_shift(1))  29.7 us
    all_to_all x3, starting transfers between devices, exchange(): lax.all_to_all(blocks, 'seq', 0, 0, axis_index_groups=groups, tiled=True)  15.8 us
    ppermute x18, starting transfers between devices, up(): return lax.ppermute(block, 'head', head_shift(1))  14.9 us
    ppermute x24, waiting for transfers between devices, send_blocks(): return [lax.ppermute(b, 'seq', shift(k)) for b, k in zip(blocks, ORDER[:3])]  12.2 us
    ppermute x18, waiting for transfers between devices, down(): return lax.ppermute(block, 'head', head_shift(SIDE - 1))  11.1 us
  transfers between devices with their start and end apart: 78, of which 32 were waited for; matrix products, arithmetic and copies ran while one was open for 3% of the time, Pallas kernels for 30%

commit v1 on v0

--- a/solution.py
+++ b/solution.py
@@ -566,7 +566,7 @@
         (2,),
         [info],
         [(g,) for g, _ in pairs]
-        + [(w, (PART, w.shape[1]), by_row(j)) for _, w in pairs for j in range(2)]
+        + [(in_hbm(w), (PART, w.shape[1]), by_row(j)) for _, w in pairs for j in range(2)]
         + [(gain, (1, PART), by_col(j)) for j in range(2)]
         + [(low, (ROWS, PART), by_col(j)) for j in range(2)],
         block_outs(EXTRA) + [((EXTRA, PART), F32)],
@@ -877,11 +877,6 @@
     )[0]
 
 
-PLANE = [
-    [seq_index(x, y, c) for x in range(SIDE) for y in range(SIDE)] for c in range(CORES)
-]
-
-
 def axis_groups(along_x):
     if along_x:
         return [
@@ -901,55 +896,41 @@
 
 def weight_mid(name, blocks, gains, tokens=()):
     count, rows, width = blocks.shape
-    step = width // 2
     part = rows // SIDE
-    gains = jnp.pad(gains, ((0, EXTRA - gains.shape[0]), (0, step - gains.shape[1])))
+    gains = jnp.pad(gains, ((0, EXTRA - gains.shape[0]), (0, 0)))
 
     def body(blocks, gains, out):
         total = blocks[0].astype(F32)
         for k in range(1, count):
             total = total + blocks[k].astype(F32)
         for y in range(SIDE):
-            out[y, :part] = total[y * part : (y + 1) * part].astype(BF16)
-            out[y, part:] = gains[...].astype(BF16)
+            out[y, :, :width] = total[y * part : (y + 1) * part].astype(BF16)
+            out[y, :EXTRA, width:] = gains[...].astype(BF16)
+            out[y, EXTRA:, width:] = jnp.zeros((part - EXTRA, PART), BF16)
 
     return call(
         name,
         body,
-        (2,),
+        (1,),
         [],
-        [(blocks, (count, rows, step), lambda i, *_: (0, 0, i)), (gains,)],
-        [
-            (
-                (SIDE, part + EXTRA, width),
-                BF16,
-                (SIDE, part + EXTRA, step),
-                lambda i, *_: (0, 0, i),
-            )
-        ],
+        [(blocks,), (gains,)],
+        [((SIDE, part, width + PART), BF16)],
         tokens,
         keep=True,
     )[0]
 
 
 def weight_sum(name, blocks, parts, tokens=()):
-    count, rows, width = blocks.shape
-    extra = rows - 64
-
     def body(blocks, *outs):
         at = 0
         for out, part in zip(outs, parts):
             cols = slice(at, at + part)
-            total = blocks[0, :64, cols].astype(F32)
-            for k in range(1, count):
-                total = total + blocks[k, :64, cols].astype(F32)
+            rows = slice(0, out.shape[0])
+            total = blocks[0, rows, cols].astype(F32)
+            for k in range(1, blocks.shape[0]):
+                total = total + blocks[k, rows, cols].astype(F32)
             out[...] = total
             at += part
-        if extra:
-            total = blocks[0, 64:, :PART].astype(F32)
-            for k in range(1, count):
-                total = total + blocks[k, 64:, :PART].astype(F32)
-            outs[-1][...] = total
 
     return call(
         name,
@@ -957,10 +938,9 @@
         (1,),
         [],
         [(blocks,)],
-        [((64, part), F32) for part in parts] + ([((extra, PART), F32)] if extra else []),
-        tokens,
-    )
-
+        [((64, part), F32) for part in parts[:-1]] + [((EXTRA, parts[-1]), F32)],
+        tokens,
+    )
 
 def weight_own_y(name, info, left, rights, arrived, tokens=()):
     n = len(rights)
@@ -1032,7 +1012,20 @@
     )
 
 
-def last_sum(name, base, received, parts):
+def plain_mid(name, blocks, tokens=()):
+    def body(blocks, out):
+        total = blocks[0].astype(F32)
+        for k in range(1, blocks.shape[0]):
+            total = total + blocks[k].astype(F32)
+        out[...] = total.astype(BF16)
+
+    shape = blocks.shape[1:]
+    return call(
+        name, body, (1,), [], [(blocks,)], [(shape, BF16)], tokens, keep=True
+    )[0]
+
+
+def last_sum(name, base, received, parts, tokens=()):
     def body(base, a, b, c, *outs):
         at = 0
         for out in outs:
@@ -1047,6 +1040,7 @@
         [],
         [(base,)] + [(r,) for r in received],
         [((64, w), F32) for w in parts],
+        tokens,
     )
 
 
@@ -1259,7 +1253,7 @@
         (feed_total,),
     )
     g_parts = ring_gather(half_a, half_b)
-    feed_blocks = exchange(feed_total, PLANE)
+    feed_blocks = exchange(feed_total, axis_groups(True))
 
     branch, grad_gate, kept, own, give = back_mix(
         info, g_parts, wo, gate, grouped, ginv, query, arrival, (feed_total,)
@@ -1289,15 +1283,21 @@
 
     feed = matmul_cols("feed_down", hidden, w2, BF16, (mix_other,), 1024)
     fed = lax.psum_scatter(feed, "head", scatter_dimension=1, tiled=True)
+    pin(fed)
 
     far_mine, far_sibling = state_scan(
         info, behind, own, give, True, "_b",
         (lambda: (feed, feed_blocks), fill_own, lambda token: (), lambda token: (fed,)),
     )
     mix_x = exchange(gated(made["own"], (far_mine,)), axis_groups(True))
+    feed_mid = plain_mid("feed_mid", feed_blocks, (far_mine,))
+    feed_grad = lax.psum_scatter(
+        feed_mid, "seq", scatter_dimension=0, axis_index_groups=axis_groups(False), tiled=True
+    )
+    pin(feed_grad)
     grad_key, grad_value = key_value_back(
         info, far_mine, far_sibling, key, value, departure, near_key, near_value, cosine, sine,
-        (),
+        (feed_mid,),
     )
     kv_other = weight_half(
         "kv_other", [(low1_other, [grad_key, grad_value])]
@@ -1306,7 +1306,7 @@
     *blocks, sums = back_blocks(
         "back_proj", info,
         [(grad_query, wq), (grad_gate, wg), (grad_key, wk), (grad_value, wv)],
-        gain1, low1, (kv_other, feed_blocks),
+        gain1, low1, (kv_other,),
     )
     pieces, sent = ring_scatter(*blocks[:6])
     kv_blocks = weight_own_y(
@@ -1320,11 +1320,11 @@
     keys, vals = HEADS * KEY, HEADS * VAL
     kv_sent = send_blocks(kv_blocks[:3], False)
     kv_half = phase_sum("kv_mid", info, X_AT, kv_blocks[3], kv_sent)
-    gains = sum_core_x(jnp.concatenate([gain1_grad, gain2_grad], axis=0), (mix_x,))
+    gains = sum_core_x(jnp.concatenate([gain1_grad, gain2_grad], axis=0), (mix_x, feed_grad))
     mix_half = weight_mid("mix_mid", mix_x, gains)
-    grad_w2, grad_w1 = weight_sum("feed_sum", feed_blocks, [vals, vals], (mix_half,))
+    feed_grad = feed_grad.astype(F32)
     grad_wo, grad_wg, grad_wq, gains = weight_sum(
-        "mix_sum", exchange(mix_half, axis_groups(False)), [vals, vals, keys]
+        "mix_sum", exchange(mix_half, axis_groups(False)), [vals, vals, keys, PART]
     )
     grad_wk, grad_wv = last_sum(
         "kv_sum", kv_half[3], send_blocks(kv_half[:3], True), (keys, vals)
@@ -1340,8 +1340,8 @@
         grad_wg,
         grad_wo.T,
         gains[1],
-        grad_w1,
-        grad_w2.T,
+        feed_grad[:, vals:],
+        feed_grad[:, :vals].T,
     )
 
 

time: 392 us -> 391 us (level)
  waiting for transfers between devices: 73.9 us -> 66.8 us
  Pallas kernels: 144 us -> 148 us
    all_to_all x3, waiting for transfers between devices: 10.6 us -> 1.15 us  [exchange(): lax.all_to_all(blocks, 'seq', 0, 0, axis_index_groups=groups, tiled=True)]
    ppermute x24, waiting for transfers between devices: 12.2 us -> 21.1 us  [send_blocks(): return [lax.ppermute(b, 'seq', shift(k)) for b, k in zip(blocks, ORDER[:3])]]
    ppermute x18, waiting for transfers between devices: 11.1 us -> 3.39 us  [down(): return lax.ppermute(block, 'head', head_shift(SIDE - 1))]
    pallas_call x40, Pallas kernels: 144 us -> 148 us  [call(): pl.pallas_call(run, name=name, grid_spec=pltpu.PrefetchScalarGridSpec(num...]
  transfers between devices with their start and end apart: 78 -> 79, of which waited for: 32 -> 31; matrix products, arithmetic and copies ran while one was open for 3% -> 3% of each run, Pallas kernels for 30% -> 31%
where the time goes in v1:
time: 391 us; the launch traced here: 385 us
  Pallas kernels  148 us (38%)
  starting transfers between devices  138 us (35%)
  waiting for transfers between devices  66.8 us (17%)
  between operations  16.4 us (4%)
  other arithmetic  9.66 us (2%)
  local copies, waits for them, and re-layouts  5.56 us (1%)
    pallas_call x40, Pallas kernels, call(): pl.pallas_call(run, name=name, grid_spec=pltpu.PrefetchScalarGridSpec(num...  148 us
    ppermute x18, starting transfers between devices, down(): return lax.ppermute(block, 'head', head_shift(SIDE - 1))  56 us
    ppermute x24, starting transfers between devices, send_blocks(): return [lax.ppermute(b, 'seq', shift(k)) for b, k in zip(blocks, ORDER[:3])]  44.8 us
    ppermute x18, waiting for transfers between devices, up(): return lax.ppermute(block, 'head', head_shift(1))  31.4 us
    ppermute x24, waiting for transfers between devices, send_blocks(): return [lax.ppermute(b, 'seq', shift(k)) for b, k in zip(blocks, ORDER[:3])]  21.1 us
    all_to_all x3, starting transfers between devices, exchange(): lax.all_to_all(blocks, 'seq', 0, 0, axis_index_groups=groups, tiled=True)  14.7 us
    ppermute x18, starting transfers between devices, up(): return lax.ppermute(block, 'head', head_shift(1))  12.9 us
  transfers between devices with their start and end apart: 79, of which 31 were waited for; matrix products, arithmetic and copies ran while one was open for 3% of the time, Pallas kernels for 31%

profile of v1, /device:TPU:0, one launch (start us, length us, event | category | flops | bytes accessed | tf_op | source)
XLA Modules:
  0.0 384.6 jit_solution(12709753546808460799)
XLA Ops:
  28.8 4.4 %collective-permute-done.3.refs_5_ = bf16[256,512]{1,0:T(8,128)(2,1)S(1)} collective-permute-done((bf16[256,512]{1,0:T(8,128)(2,1)S(1)}, bf16[256,512]{1,0:T(8,128)(2,1)S(1)}, u32[]{:S(2)}, u32[]{:S(2)}) %collective-permute-start.3) | collective-permute-done | bytes 262176 | tf_op jit(solution)/shard_map/ppermute | solution.py:48
  36.8 4.4 %collective-permute-start.8 = (bf16[512,512]{1,0:T(8,128)(2,1)S(1)}, bf16[512,512]{1,0:T(8,128)(2,1)S(1)}, u32[]{:S(2)}, u32[]{:S(2)}) collective-permute-start(bf16[512,512]{1,0:T(8,128)(2,1)S(1)} %get-tuple-element.129.refs_1_), channel_id=1, source_target_pairs={{0,2},{1,3},{2,0},{3,1},{4,6},{5,7},{6,4},{7,5},{8,10},{9,11},{10,... | collective-permute-start | bytes 1572872 | tf_op jit(solution)/shard_map/ppermute | solution.py:95
  41.2 6.3 %key_value.1 = (bf16[512,512]{1,0:T(8,128)(2,1)}, bf16[512,1024]{1,0:T(8,128)(2,1)}, f32[256,512]{1,0:T(8,128)S(1)}, bf16[256,512]{1,0:T(8,128)(2,1)S(1)}) custom-call(s32[8]{0:T(128)S(1)} %stack.35.refs_6_.refs_0_, bf16[512,2048]{1,0:T(8,128)(2,1)S(1)} %get-tuple-element.121.refs_1_.refs_0_.refs_15_.refs_16_, bf16[2048,512]{1,0:T(8,128)(2,1)S(1)} %copy-done.5, ...), custom_call_target="tpu_custom_call" | custom-call | flops 8800000000 | tf_op jit(solution)/shard_map/key_value/pallas_call | solution.py:192
  47.6 6.0 %query_part.1 = (bf16[512,512]{1,0:T(8,128)(2,1)}, bf16[2,512,512]{2,1,0:T(8,128)(2,1)}, f32[512,1024]{1,0:T(8,128)S(1)}) custom-call(bf16[512,2048]{1,0:T(8,128)(2,1)S(1)} %get-tuple-element.121.refs_1_.refs_0_.refs_15_.refs_16_, bf16[2048,512]{1,0:T(8,128)(2,1)S(1)} %copy-done.4, bf16[512,512]{1,0:T(8,128)(2,1)} %get-tuple-element.122.refs_2_.refs_4_.refs_3_, ...), custom_call_target="tpu_custom_call" | custom-call | flops 6600000000 | tf_op jit(solution)/shard_map/query_part/pallas_call | solution.py:192
  87.3 6.9 %mix.1 = (bf16[512,1024]{1,0:T(8,128)(2,1)}, bf16[512,1024]{1,0:T(8,128)(2,1)}, f32[2,512,1]{2,1,0:T(8,128)S(1)}, bf16[256,512]{1,0:T(8,128)(2,1)S(1)}, bf16[256...) custom-call(s32[8]{0:T(128)S(1)} %stack.35.refs_6_.refs_0_, ...), custom_call_target="tpu_custom_call" | custom-call | flops 9900000256 | tf_op jit(solution)/shard_map/mix/pallas_call | solution.py:192
  118.5 8.6 %collective-permute-start.27 = (bf16[256,512]{1,0:T(8,128)(2,1)S(1)}, bf16[256,512]{1,0:T(8,128)(2,1)S(1)}, u32[]{:S(2)}, u32[]{:S(2)}) collective-permute-start(bf16[256,512]{1,0:T(8,128)(2,1)S(1)} %get-tuple-element.150.refs_3_), channel_id=1, source_target_pairs={{0,1},{1,2},{2,3},{3,0},{4,5},{5,6},{6,7},{7,4},{8,9},{9,10},{10,1... | collective-permute-start | bytes 786440 | tf_op jit(solution)/shard_map/ppermute | solution.py:48
  133.5 4.0 %collective-permute-done.27.refs_5_ = bf16[256,512]{1,0:T(8,128)(2,1)S(1)} collective-permute-done((bf16[256,512]{1,0:T(8,128)(2,1)S(1)}, bf16[256,512]{1,0:T(8,128)(2,1)S(1)}, u32[]{:S(2)}, u32[]{:S(2)}) %collective-permute-start.27) | collective-permute-done | bytes 262176 | tf_op jit(solution)/shard_map/ppermute | solution.py:48
  140.8 7.5 %feed_up.1 = (bf16[512,2048]{1,0:T(8,128)(2,1)S(1)}, f32[512,1]{1,0:T(8,128)}, f32[512,1]{1,0:T(8,128)}, f32[512,512]{1,0:T(8,128)}, bf16[512,1024]{1,0:T(8,128)(2,1)S(1)}, /*index=5*/bf16[512,1024]{1,0:T(8,128)(2,1)S(1)}) custom-call(s32[8]{0:T(128)S(1)} %stack.35.refs_6_.refs_0_, bf16[4,512,512]{2,1,0:T(8,128)(2,1)} %get-tuple-element.120.refs_1_, ...), custom_call_target="tpu_custom_call" | custom-call | flops 12099999744 | tf_op jit(solution)/shard_map/feed_up/pallas_call | solution.py:192
  153.8 7.1 %back_feed.1 = (bf16[272,512]{1,0:T(8,128)(2,1)S(1)}, bf16[256,512]{1,0:T(8,128)(2,1)S(1)}, bf16[272,512]{1,0:T(8,128)(2,1)S(1)}, bf16[256,512]{1,0:T(8,128)(2,1...) custom-call(s32[8]{0:T(128)S(1)} %stack.35.refs_6_.refs_0_, ...), custom_call_target="tpu_custom_call" | custom-call | flops 7699999744 | tf_op jit(solution)/shard_map/back_feed/pallas_call | solution.py:192
  179.6 5.0 %all-to-all-start = ((bf16[4,256,2048]{2,1,0:T(8,128)(2,1)}), bf16[4,256,2048]{2,1,0:T(8,128)(2,1)}, u32[]{:S(2)}, u32[]{:S(2)}) async-start(bf16[4,256,2048]{2,1,0:T(8,128)(2,1)} %bitcast.46), calls=%async_computation.1 | async-start | bytes 8388608 | tf_op jit(solution)/shard_map/all_to_all | solution.py:892
  185.4 4.4 %norm_back2.1 = (f32[512,512]{1,0:T(8,128)}, f32[1,512]{1,0:T(1,128)S(1)}, bf16[256,512]{1,0:T(8,128)(2,1)S(1)}, bf16[256,512]{1,0:T(8,128)(2,1)S(1)}) custom-call(s32[8]{0:T(128)S(1)} %stack.35.refs_6_.refs_0_, f32[512,512]{1,0:T(8,128)} %get-tuple-element.158.refs_1_, f32[16,512]{1,0:T(8,128)S(1)} %get-tuple-element.159.refs_2_, ...), custom_call_target="tpu_custom_call" | custom-call | flops 109999996928 | tf_op jit(solution)/shard_map/norm_back2/pallas_call | solution.py:192
  209.2 7.0 %back_mix.1 = (bf16[512,2048]{1,0:T(8,128)(2,1)S(1)}, bf16[512,1024]{1,0:T(8,128)(2,1)}, bf16[512,1024]{1,0:T(8,128)(2,1)}, f32[256,512]{1,0:T(8,128)S(1)}, bf16[256,512]{1,0:T(8,128)(2,1)S(1)}) custom-call(s32[8]{0:T(128)S(1)} %stack.35.refs_6_.refs_0_, bf16[256,512]{1,0:T(8,128)(2,1)S(1)} %get-tuple-element.168.refs_1_, ...), custom_call_target="tpu_custom_call" | custom-call | flops 6600000000 | tf_op jit(solution)/shard_map/back_mix/pallas_call | solution.py:192
  218.9 5.9 %retain_back.1 = (bf16[512,512]{1,0:T(8,128)(2,1)}, f32[512,512]{1,0:T(8,128)}, f32[512,1024]{1,0:T(8,128)}) custom-call(s32[8]{0:T(128)S(1)} %stack.35.refs_6_.refs_0_, bf16[512,1024]{1,0:T(8,128)(2,1)} %get-tuple-element.178.refs_1_, bf16[512,1024]{1,0:T(8,128)(2,1)} %get-tuple-element.123.refs_3_.refs_2_.refs_4_, ...), custom_call_target="tpu_custom_call" | custom-call | flops 660000000 | tf_op jit(solution)/shard_map/retain_back/pallas_call | solution.py:192
  224.8 6.8 %mix_other.1.refs_2_ = bf16[1024,2560]{1,0:T(8,128)(2,1)} custom-call(bf16[1024,512]{1,0:T(8,128)(2,1)} %bitcast.51, bf16[1024,512]{1,0:T(8,128)(2,1)} %bitcast.47, bf16[512,1024]{1,0:T(8,128)(2,1)} %get-tuple-element.176.refs_2_, bf16[512,1024]{1,0:T(8,128)(2,1)} %get-tuple-element.177.refs_3_.refs_2_, ...), custom_call_target="tpu_custom_call" | custom-call | flops 198000000 | tf_op jit(solution)/shard_map/mix_other/pallas_call | solution.py:192
  241.0 7.5 %mix_own.1.refs_5_.refs_0_ = bf16[1024,2560]{1,0:T(8,128)(2,1)} custom-call(bf16[1024,512]{1,0:T(8,128)(2,1)} %bitcast.50, bf16[1024,512]{1,0:T(8,128)(2,1)} %bitcast.45, bf16[512,1024]{1,0:T(8,128)(2,1)} %get-tuple-element.176.refs_2_, bf16[512,1024]{1,0:T(8,128)(2,1)} %get-tuple-element.177.refs_3_.refs_2_, ...), custom_call_target="tpu_custom_call" | custom-call | flops 1100000000 | tf_op jit(solution)/shard_map/mix_own/pallas_call | solution.py:192
  268.2 5.2 %all-to-all-start.1 = ((bf16[4,256,2560]{2,1,0:T(8,128)(2,1)}), bf16[4,256,2560]{2,1,0:T(8,128)(2,1)}, u32[]{:S(2)}, u32[]{:S(2)}) async-start(bf16[4,256,2560]{2,1,0:T(8,128)(2,1)} %bitcast.43), calls=%async_computation.2 | async-start | bytes 10485760 | tf_op jit(solution)/shard_map/all_to_all | solution.py:892
  277.3 4.3 %key_value_back.1 = (bf16[512,512]{1,0:T(8,128)(2,1)}, bf16[512,1024]{1,0:T(8,128)(2,1)}) custom-call(s32[8]{0:T(128)S(1)} %stack.35.refs_6_.refs_0_, bf16[256,512]{1,0:T(8,128)(2,1)S(1)} %copy-done.18, bf16[256,512]{1,0:T(8,128)(2,1)S(1)} %collective-permute-done.56.refs_2_, bf16[512,512]{1,0:T(8,128)(2,1)} %get-tuple-element.122.refs_2_.refs_4_.refs_3_, ...), custom_call_target="tpu_custom_call" | custom-call | flops 109999996928 | tf_op jit(solution)/shard_map/key_value_back/pallas_call | solution.py:192
  281.6 4.9 %kv_other.1.refs_17_ = bf16[1024,1536]{1,0:T(8,128)(2,1)} custom-call(bf16[1024,512]{1,0:T(8,128)(2,1)} %bitcast.48, bf16[512,512]{1,0:T(8,128)(2,1)} %get-tuple-element.195.refs_1_.refs_3_, bf16[512,1024]{1,0:T(8,128)(2,1)} %get-tuple-element.196.refs_2_.refs_4_), custom_call_target="tpu_custom_call" | custom-call | flops 990000000 | tf_op jit(solution)/shard_map/kv_other/pallas_call | solution.py:192
  287.0 13.5 %back_proj.1 = (bf16[272,512]{1,0:T(8,128)(2,1)S(1)}, bf16[256,512]{1,0:T(8,128)(2,1)S(1)}, bf16[272,512]{1,0:T(8,128)(2,1)S(1)}, bf16[256,512]{1,0:T(8,128)(2,1...) custom-call(s32[8]{0:T(128)S(1)} %stack.35.refs_6_.refs_0_, ...), custom_call_target="tpu_custom_call" | custom-call | flops 110000000 | tf_op jit(solution)/shard_map/back_proj/pallas_call | solution.py:192
  307.0 4.3 %collective-permute-done.57 = bf16[272,512]{1,0:T(8,128)(2,1)S(1)} collective-permute-done((bf16[272,512]{1,0:T(8,128)(2,1)S(1)}, bf16[272,512]{1,0:T(8,128)(2,1)S(1)}, u32[]{:S(2)}, u32[]{:S(2)}) %collective-permute-start.57) | collective-permute-done | bytes 278560 | tf_op jit(solution)/shard_map/ppermute | solution.py:48
  314.8 7.1 %kv_own.1 = (bf16[256,1536]{1,0:T(8,128)(2,1)S(1)}, bf16[256,1536]{1,0:T(8,128)(2,1)}, bf16[256,1536]{1,0:T(8,128)(2,1)}, f32[256,1536]{1,0:T(8,128)S(1)}) custom-call(s32[8]{0:T(128)S(1)} %stack.35.refs_6_.refs_0_, bf16[4,4,64,512]{3,2,1,0:T(8,128)(2,1)} %get-tuple-element.148.refs_1_.refs_2_, bf16[4,4,64,512]{3,2,1,0:T(8,128)(2,1)} %get-tuple-element.148.refs_1_.refs_2_, ...), custom_call_target="tpu_custom_call" | custom-call | flops 110000000 | tf_op jit(solution)/shard_map/kv_own/pallas_call | solution.py:192
  343.2 4.3 %mix_mid.1 = bf16[4,64,3072]{2,1,0:T(8,128)(2,1)} custom-call(bf16[4,256,2560]{2,1,0:T(8,128)(2,1)} %all-to-all-done.1.refs_2_.refs_0_, f32[16,512]{1,0:T(8,128)S(1)} %pad.4.refs_1_), custom_call_target="tpu_custom_call" | custom-call | flops 110000000 | tf_op jit(solution)/shard_map/mix_mid/pallas_call | solution.py:192
  347.5 4.5 %all-to-all-start.2 = ((bf16[4,64,3072]{2,1,0:T(8,128)(2,1)}), bf16[4,64,3072]{2,1,0:T(8,128)(2,1)}, u32[]{:S(2)}, u32[]{:S(2)}) async-start(bf16[4,64,3072]{2,1,0:T(8,128)(2,1)} %mix_mid.1), calls=%async_computation.4 | async-start | bytes 3145728 | tf_op jit(solution)/shard_map/all_to_all | solution.py:892
  352.0 7.7 %collective-permute-done.69.refs_3_ = bf16[256,1536]{1,0:T(8,128)(2,1)} collective-permute-done((bf16[256,1536]{1,0:T(8,128)(2,1)}, bf16[256,1536]{1,0:T(8,128)(2,1)}, u32[]{:S(2)}, u32[]{:S(2)}) %collective-permute-start.69) | collective-permute-done | bytes 786464 | tf_op jit(solution)/shard_map/ppermute | solution.py:1053
  (310 shorter events, 220.7 us)
Async XLA Ops:
  8.3 20.5 %collective-permute-start.1 = (bf16[256,512]{1,0:T(8,128)(2,1)S(1)}, bf16[256,512]{1,0:T(8,128)(2,1)S(1)}, u32[]{:S(2)}, u32[]{:S(2)}) collective-permute-start(bf16[256,512]{1,0:T(8,128)(2,1)S(1)} %get-tuple-element.227.refs_2_), channel_id=1, source_target_pairs={{0,1},{1,2},{2,3},{3,0},{4,5},{5,6},{6,7},{7,4},{8,9},{9,10},{10,1... | collective-permute-start | bytes 786440 | tf_op jit(solution)/shard_map/ppermute | solution.py:48
  36.8 22.1 %collective-permute-start.7 = (bf16[512,512]{1,0:T(8,128)(2,1)S(1)}, bf16[512,512]{1,0:T(8,128)(2,1)S(1)}, u32[]{:S(2)}, u32[]{:S(2)}) collective-permute-start(bf16[512,512]{1,0:T(8,128)(2,1)S(1)} %get-tuple-element.129.refs_1_), channel_id=1, source_target_pairs={{0,1},{1,2},{2,3},{3,0},{4,5},{5,6},{6,7},{7,4},{8,9},{9,10},{10,1... | collective-permute-start | bytes 1572872 | tf_op jit(solution)/shard_map/ppermute | solution.py:95
  36.8 25.5 %collective-permute-start.8 = (bf16[512,512]{1,0:T(8,128)(2,1)S(1)}, bf16[512,512]{1,0:T(8,128)(2,1)S(1)}, u32[]{:S(2)}, u32[]{:S(2)}) collective-permute-start(bf16[512,512]{1,0:T(8,128)(2,1)S(1)} %get-tuple-element.129.refs_1_), channel_id=1, source_target_pairs={{0,2},{1,3},{2,0},{3,1},{4,6},{5,7},{6,4},{7,5},{8,10},{9,11},{10,... | collective-permute-start | bytes 1572872 | tf_op jit(solution)/shard_map/ppermute | solution.py:95
  41.2 21.1 %collective-permute-start.9 = (bf16[512,512]{1,0:T(8,128)(2,1)S(1)}, bf16[512,512]{1,0:T(8,128)(2,1)S(1)}, u32[]{:S(2)}, u32[]{:S(2)}) collective-permute-start(bf16[512,512]{1,0:T(8,128)(2,1)S(1)} %get-tuple-element.129.refs_1_), channel_id=1, source_target_pairs={{0,3},{1,0},{2,1},{3,2},{4,7},{5,4},{6,5},{7,6},{8,11},{9,8},{10,9... | collective-permute-start | bytes 1572872 | tf_op jit(solution)/shard_map/ppermute | solution.py:95
  97.4 16.6 %collective-permute-start.22 = (bf16[256,512]{1,0:T(8,128)(2,1)S(1)}, bf16[256,512]{1,0:T(8,128)(2,1)S(1)}, u32[]{:S(2)}, u32[]{:S(2)}) collective-permute-start(bf16[256,512]{1,0:T(8,128)(2,1)S(1)} %get-tuple-element.142), channel_id=1, source_target_pairs={{0,1},{1,2},{2,3},{3,0},{4,5},{5,6},{6,7},{7,4},{8,9},{9,10},{10,1... | collective-permute-start | bytes 786440 | tf_op jit(solution)/shard_map/ppermute | solution.py:48
  97.4 16.6 %collective-permute-start.23 = (bf16[256,512]{1,0:T(8,128)(2,1)S(1)}, bf16[256,512]{1,0:T(8,128)(2,1)S(1)}, u32[]{:S(2)}, u32[]{:S(2)}) collective-permute-start(bf16[256,512]{1,0:T(8,128)(2,1)S(1)} %get-tuple-element.143), channel_id=1, source_target_pairs={{0,3},{1,0},{2,1},{3,2},{4,7},{5,4},{6,5},{7,6},{8,11},{9,8},{10,9... | collective-permute-start | bytes 786440 | tf_op jit(solution)/shard_map/ppermute | solution.py:52
  118.5 19.0 %collective-permute-start.27 = (bf16[256,512]{1,0:T(8,128)(2,1)S(1)}, bf16[256,512]{1,0:T(8,128)(2,1)S(1)}, u32[]{:S(2)}, u32[]{:S(2)}) collective-permute-start(bf16[256,512]{1,0:T(8,128)(2,1)S(1)} %get-tuple-element.150.refs_3_), channel_id=1, source_target_pairs={{0,1},{1,2},{2,3},{3,0},{4,5},{5,6},{6,7},{7,4},{8,9},{9,10},{10,1... | collective-permute-start | bytes 786440 | tf_op jit(solution)/shard_map/ppermute | solution.py:48
  153.8 21.9 %collective-permute-start.38 = (bf16[1024,2048]{1,0:T(8,128)(2,1)}, bf16[1024,2048]{1,0:T(8,128)(2,1)S(1)}, u32[]{:S(2)}, u32[]{:S(2)}) collective-permute-start(bf16[1024,2048]{1,0:T(8,128)(2,1)} %feed_other.1.refs_8_), channel_id=1, source_target_pairs={{0,4},{4,0},{8,12},{12,8},{16,20},{20,16},{24,28},{28,24},{32,36},... | collective-permute-start | bytes 12582920 | tf_op jit(solution)/shard_map/ppermute | solution.py:1247
  163.8 20.8 %collective-permute-start.34 = (bf16[256,512]{1,0:T(8,128)(2,1)}, bf16[256,512]{1,0:T(8,128)(2,1)S(1)}, u32[]{:S(2)}, u32[]{:S(2)}) collective-permute-start(bf16[256,512]{1,0:T(8,128)(2,1)} %get-tuple-element.162), channel_id=1, source_target_pairs={{0,1},{1,2},{2,3},{3,0},{4,5},{5,6},{6,7},{7,4},{8,9},{9,10},{10,1... | collective-permute-start | bytes 786440 | tf_op jit(solution)/shard_map/ppermute | solution.py:48
  163.8 20.8 %collective-permute-start.35 = (bf16[272,512]{1,0:T(8,128)(2,1)S(1)}, bf16[272,512]{1,0:T(8,128)(2,1)S(1)}, u32[]{:S(2)}, u32[]{:S(2)}) collective-permute-start(bf16[272,512]{1,0:T(8,128)(2,1)S(1)} %get-tuple-element.163), channel_id=1, source_target_pairs={{0,3},{1,0},{2,1},{3,2},{4,7},{5,4},{6,5},{7,6},{8,11},{9,8},{10,9... | collective-permute-start | bytes 835592 | tf_op jit(solution)/shard_map/ppermute | solution.py:52
  179.6 56.4 %all-to-all-start = ((bf16[4,256,2048]{2,1,0:T(8,128)(2,1)}), bf16[4,256,2048]{2,1,0:T(8,128)(2,1)}, u32[]{:S(2)}, u32[]{:S(2)}) async-start(bf16[4,256,2048]{2,1,0:T(8,128)(2,1)} %bitcast.46), calls=%async_computation.1 | async-start | bytes 8388608 | tf_op jit(solution)/shard_map/all_to_all | solution.py:892
  184.6 81.8 %reduce-scatter.3.cloned.1.call-start = ((), (), s32[]{:S(2)}) async-start(), calls=%async_computation.5 | async-start | bytes 2621440 | tf_op jit(solution)/shard_map/reduce_scatter | solution.py:1285
  216.3 19.7 %collective-permute-start.45 = (bf16[256,512]{1,0:T(8,128)(2,1)S(1)}, bf16[256,512]{1,0:T(8,128)(2,1)S(1)}, u32[]{:S(2)}, u32[]{:S(2)}) collective-permute-start(bf16[256,512]{1,0:T(8,128)(2,1)S(1)} %get-tuple-element.173.refs_2_), channel_id=1, source_target_pairs={{0,4},{4,0},{8,12},{12,8},{16,20},{20,16},{24,28},{28,24},{32,36},... | collective-permute-start | bytes 786440 | tf_op jit(solution)/shard_map/ppermute | solution.py:1097
  268.2 66.3 %all-to-all-start.1 = ((bf16[4,256,2560]{2,1,0:T(8,128)(2,1)}), bf16[4,256,2560]{2,1,0:T(8,128)(2,1)}, u32[]{:S(2)}, u32[]{:S(2)}) async-start(bf16[4,256,2560]{2,1,0:T(8,128)(2,1)} %bitcast.43), calls=%async_computation.2 | async-start | bytes 10485760 | tf_op jit(solution)/shard_map/all_to_all | solution.py:892
  273.4 58.7 %reduce-scatter.5.cloned.1.call-start = ((), (), s32[]{:S(2)}) async-start(), calls=%async_computation.6 | async-start | bytes 1310720 | tf_op jit(solution)/shard_map/reduce_scatter | solution.py:1294
  286.4 28.4 %collective-permute-start.63 = (bf16[1024,1536]{1,0:T(8,128)(2,1)}, bf16[1024,1536]{1,0:T(8,128)(2,1)}, u32[]{:S(2)}, u32[]{:S(2)}) collective-permute-start(bf16[1024,1536]{1,0:T(8,128)(2,1)} %kv_other.1.refs_17_), channel_id=1, source_target_pairs={{0,4},{4,0},{8,12},{12,8},{16,20},{20,16},{24,28},{28,24},{32,36},... | collective-permute-start | bytes 9437192 | tf_op jit(solution)/shard_map/ppermute | solution.py:1305
  303.8 21.0 %collective-permute-start.59 = (bf16[256,512]{1,0:T(8,128)(2,1)S(1)}, bf16[256,512]{1,0:T(8,128)(2,1)S(1)}, u32[]{:S(2)}, u32[]{:S(2)}) collective-permute-start(bf16[256,512]{1,0:T(8,128)(2,1)S(1)} %get-tuple-element.201), channel_id=1, source_target_pairs={{0,1},{1,2},{2,3},{3,0},{4,5},{5,6},{6,7},{7,4},{8,9},{9,10},{10,1... | collective-permute-start | bytes 786440 | tf_op jit(solution)/shard_map/ppermute | solution.py:48
  303.8 21.6 %collective-permute-start.60 = (bf16[272,512]{1,0:T(8,128)(2,1)S(1)}, bf16[272,512]{1,0:T(8,128)(2,1)S(1)}, u32[]{:S(2)}, u32[]{:S(2)}) collective-permute-start(bf16[272,512]{1,0:T(8,128)(2,1)S(1)} %get-tuple-element.202), channel_id=1, source_target_pairs={{0,3},{1,0},{2,1},{3,2},{4,7},{5,4},{6,5},{7,6},{8,11},{9,8},{10,9... | collective-permute-start | bytes 835592 | tf_op jit(solution)/shard_map/ppermute | solution.py:52
  311.3 16.6 %collective-permute-start.58 = (bf16[272,512]{1,0:T(8,128)(2,1)S(1)}, bf16[272,512]{1,0:T(8,128)(2,1)S(1)}, u32[]{:S(2)}, u32[]{:S(2)}) collective-permute-start(bf16[272,512]{1,0:T(8,128)(2,1)S(1)} %add_convert_fusion.1.refs_7_), channel_id=1, source_target_pairs={{0,1},{1,2},{2,3},{3,0},{4,5},{5,6},{6,7},{7,4},{8,9},{9,10},{10,1... | collective-permute-start | bytes 835592 | tf_op jit(solution)/shard_map/ppermute | solution.py:48
  311.5 16.5 %collective-permute-start.62 = (bf16[256,512]{1,0:T(8,128)(2,1)S(1)}, bf16[256,512]{1,0:T(8,128)(2,1)S(1)}, u32[]{:S(2)}, u32[]{:S(2)}) collective-permute-start(bf16[256,512]{1,0:T(8,128)(2,1)S(1)} %add_convert_fusion.3.refs_8_), channel_id=1, source_target_pairs={{0,3},{1,0},{2,1},{3,2},{4,7},{5,4},{6,5},{7,6},{8,11},{9,8},{10,9... | collective-permute-start | bytes 786440 | tf_op jit(solution)/shard_map/ppermute | solution.py:52
  321.9 30.1 %collective-permute-start.68 = (bf16[256,1536]{1,0:T(8,128)(2,1)S(1)}, bf16[256,1536]{1,0:T(8,128)(2,1)S(1)}, u32[]{:S(2)}, u32[]{:S(2)}) collective-permute-start(bf16[256,1536]{1,0:T(8,128)(2,1)S(1)} %get-tuple-element.208.refs_12_), channel_id=1, source_target_pairs={{0,16},{4,20},{8,24},{12,28},{16,0},{20,4},{24,8},{28,12},{32,48},... | collective-permute-start | bytes 2359304 | tf_op jit(solution)/shard_map/ppermute | solution.py:1053
  324.7 35.0 %collective-permute-start.69 = (bf16[256,1536]{1,0:T(8,128)(2,1)}, bf16[256,1536]{1,0:T(8,128)(2,1)}, u32[]{:S(2)}, u32[]{:S(2)}) collective-permute-start(bf16[256,1536]{1,0:T(8,128)(2,1)} %get-tuple-element.215), channel_id=1, source_target_pairs={{0,8},{4,12},{8,16},{12,20},{16,24},{20,28},{24,0},{28,4},{32,40},... | collective-permute-start | bytes 2359304 | tf_op jit(solution)/shard_map/ppermute | solution.py:1053
  325.3 35.4 %collective-permute-start.70 = (bf16[256,1536]{1,0:T(8,128)(2,1)}, bf16[256,1536]{1,0:T(8,128)(2,1)}, u32[]{:S(2)}, u32[]{:S(2)}) collective-permute-start(bf16[256,1536]{1,0:T(8,128)(2,1)} %get-tuple-element.216), channel_id=1, source_target_pairs={{0,24},{4,28},{8,0},{12,4},{16,8},{20,12},{24,16},{28,20},{32,56},... | collective-permute-start | bytes 2359304 | tf_op jit(solution)/shard_map/ppermute | solution.py:1053
  347.5 27.2 %all-to-all-start.2 = ((bf16[4,64,3072]{2,1,0:T(8,128)(2,1)}), bf16[4,64,3072]{2,1,0:T(8,128)(2,1)}, u32[]{:S(2)}, u32[]{:S(2)}) async-start(bf16[4,64,3072]{2,1,0:T(8,128)(2,1)} %mix_mid.1), calls=%async_computation.4 | async-start | bytes 3145728 | tf_op jit(solution)/shard_map/all_to_all | solution.py:892
  (97 other events, 1067.8 us)
Sparse Core Ops, SparseCore 0:
  236.1 30.2 reduce-scatter.2
  287.1 24.0 reduce-scatter.4

commit v2 on v1

--- a/solution.py
+++ b/solution.py
@@ -1056,11 +1056,11 @@
 X_AT, Y_AT = 6, 7
 
 
-def scan_weights(decay, place, reverse):
+def scan_weights(log_decay, place, reverse):
     x, y, _ = place
     rel = jnp.arange(SIDE)
-    origin = lax.rem(y - rel + SIDE, SIDE)
-    target = lax.rem(y + rel, SIDE)
+    origin = (y - rel) & 3
+    target = (y + rel) & 3
     hops = jnp.arange(1, SIDE)
     if reverse:
         row = origin
@@ -1075,8 +1075,9 @@
     gap = gap.reshape(-1)
     power = jnp.concatenate([row, before, jnp.maximum(gap - 1, 0), carry]).astype(F32)
     keep = jnp.concatenate([row >= 0, counts, gap > 0, carry >= 0]).astype(F32)
-    values = keep * jnp.exp(2.0 * jnp.log(decay) * power)
-    return jnp.concatenate([decay[None], values, jnp.zeros((4,), F32)])
+    power = jnp.concatenate([jnp.full((1,), 0.5, F32), power, jnp.zeros((4,), F32)])
+    keep = jnp.concatenate([jnp.ones((1,), F32), keep, jnp.zeros((4,), F32)])
+    return keep * jnp.exp(2.0 * log_decay * power)
 
 
 W_ROW, W_BEFORE, W_ANSWER, W_CARRY = 1, 5, 8, 24
@@ -1161,15 +1162,11 @@
 def shards(layer_in, gain1, wq, wk, wv, wg, wo, gain2, w1, w2, starts, cotangent):
     seq_rank = lax.axis_index("seq")
     head_rank = lax.axis_index("head")
-    x, y, core = (
-        seq_rank // (SIDE * CORES),
-        (seq_rank // CORES) % SIDE,
-        seq_rank % CORES,
-    )
+    x, y, core = seq_rank >> 3, (seq_rank >> 1) & 3, seq_rank & 1
     place = (x, y, core)
     PINNED.clear()
     info = jnp.stack(
-        [head_rank, core] + [(head_rank + k) % SIDE for k in ORDER] + [x, y]
+        [head_rank, core] + [(head_rank + k) & 3 for k in ORDER] + [x, y]
     ).astype(jnp.int32)
     gain1, gain2 = gain1[None], gain2[None]
 
@@ -1199,9 +1196,10 @@
     ).astype(F32)
     arrival, departure = arrival[:, :, None], departure[:, :, None]
     pin(decay)
-    rank_decay = lax.dynamic_index_in_dim(jnp.exp(ROWS * log_decay), core, 0, False)
-    ahead = scan_weights(rank_decay, place, False)
-    behind = scan_weights(rank_decay, place, True)
+    own_head = (head_rank * HEADS + core).astype(F32)
+    rank_log = ROWS * jnp.log1p(-jnp.exp2(-5.0 - own_head))
+    ahead = scan_weights(rank_log, place, False)
+    behind = scan_weights(rank_log, place, True)
 
     tables = (arrival, departure, ahead, behind, info)
     x_parts = ring_gather(

time: 391 us -> 391 us (level)
  no operation moved by 1% of the time
where the time goes in v2:
time: 391 us; the launch traced here: 385 us
  Pallas kernels  148 us (38%)
  starting transfers between devices  138 us (35%)
  waiting for transfers between devices  68.5 us (18%)
  between operations  15.8 us (4%)
  other arithmetic  9.14 us (2%)
  local copies, waits for them, and re-layouts  4.97 us (1%)
    pallas_call x40, Pallas kernels, call(): pl.pallas_call(run, name=name, grid_spec=pltpu.PrefetchScalarGridSpec(num...  148 us
    ppermute x18, starting transfers between devices, down(): return lax.ppermute(block, 'head', head_shift(SIDE - 1))  56 us
    ppermute x24, starting transfers between devices, send_blocks(): return [lax.ppermute(b, 'seq', shift(k)) for b, k in zip(blocks, ORDER[:3])]  44.8 us
    ppermute x18, waiting for transfers between devices, up(): return lax.ppermute(block, 'head', head_shift(1))  33.1 us
    ppermute x24, waiting for transfers between devices, send_blocks(): return [lax.ppermute(b, 'seq', shift(k)) for b, k in zip(blocks, ORDER[:3])]  21.1 us
    all_to_all x3, starting transfers between devices, exchange(): lax.all_to_all(blocks, 'seq', 0, 0, axis_index_groups=groups, tiled=True)  14.7 us
    ppermute x18, starting transfers between devices, up(): return lax.ppermute(block, 'head', head_shift(1))  12.9 us
  transfers between devices with their start and end apart: 79, of which 31 were waited for; matrix products, arithmetic and copies ran while one was open for 3% of the time, Pallas kernels for 31%

profile of v2, /device:TPU:0, one launch (start us, length us, event | category | flops | bytes accessed | tf_op | source)
XLA Modules:
  0.0 384.6 jit_solution(2353236347221221134)
XLA Ops:
  28.8 4.4 %collective-permute-done.3.refs_5_ = bf16[256,512]{1,0:T(8,128)(2,1)S(1)} collective-permute-done((bf16[256,512]{1,0:T(8,128)(2,1)S(1)}, bf16[256,512]{1,0:T(8,128)(2,1)S(1)}, u32[]{:S(2)}, u32[]{:S(2)}) %collective-permute-start.3) | collective-permute-done | bytes 262176 | tf_op jit(solution)/shard_map/ppermute | solution.py:48
  36.8 4.4 %collective-permute-start.8 = (bf16[512,512]{1,0:T(8,128)(2,1)S(1)}, bf16[512,512]{1,0:T(8,128)(2,1)S(1)}, u32[]{:S(2)}, u32[]{:S(2)}) collective-permute-start(bf16[512,512]{1,0:T(8,128)(2,1)S(1)} %get-tuple-element.129.refs_1_), channel_id=1, source_target_pairs={{0,2},{1,3},{2,0},{3,1},{4,6},{5,7},{6,4},{7,5},{8,10},{9,11},{10,... | collective-permute-start | bytes 1572872 | tf_op jit(solution)/shard_map/ppermute | solution.py:95
  41.2 6.3 %key_value.1 = (bf16[512,512]{1,0:T(8,128)(2,1)}, bf16[512,1024]{1,0:T(8,128)(2,1)}, f32[256,512]{1,0:T(8,128)S(1)}, bf16[256,512]{1,0:T(8,128)(2,1)S(1)}) custom-call(s32[8]{0:T(128)S(1)} %stack.35.refs_6_.refs_0_, bf16[512,2048]{1,0:T(8,128)(2,1)S(1)} %get-tuple-element.121.refs_1_.refs_0_.refs_15_.refs_16_, bf16[2048,512]{1,0:T(8,128)(2,1)S(1)} %copy-done.5, ...), custom_call_target="tpu_custom_call" | custom-call | flops 8800000000 | tf_op jit(solution)/shard_map/key_value/pallas_call | solution.py:192
  47.6 6.0 %query_part.1 = (bf16[512,512]{1,0:T(8,128)(2,1)}, bf16[2,512,512]{2,1,0:T(8,128)(2,1)}, f32[512,1024]{1,0:T(8,128)S(1)}) custom-call(bf16[512,2048]{1,0:T(8,128)(2,1)S(1)} %get-tuple-element.121.refs_1_.refs_0_.refs_15_.refs_16_, bf16[2048,512]{1,0:T(8,128)(2,1)S(1)} %copy-done.4, bf16[512,512]{1,0:T(8,128)(2,1)} %get-tuple-element.122.refs_2_.refs_4_.refs_3_, ...), custom_call_target="tpu_custom_call" | custom-call | flops 6600000000 | tf_op jit(solution)/shard_map/query_part/pallas_call | solution.py:192
  87.3 6.9 %mix.1 = (bf16[512,1024]{1,0:T(8,128)(2,1)}, bf16[512,1024]{1,0:T(8,128)(2,1)}, f32[2,512,1]{2,1,0:T(8,128)S(1)}, bf16[256,512]{1,0:T(8,128)(2,1)S(1)}, bf16[256...) custom-call(s32[8]{0:T(128)S(1)} %stack.35.refs_6_.refs_0_, ...), custom_call_target="tpu_custom_call" | custom-call | flops 9900000256 | tf_op jit(solution)/shard_map/mix/pallas_call | solution.py:192
  118.5 8.6 %collective-permute-start.27 = (bf16[256,512]{1,0:T(8,128)(2,1)S(1)}, bf16[256,512]{1,0:T(8,128)(2,1)S(1)}, u32[]{:S(2)}, u32[]{:S(2)}) collective-permute-start(bf16[256,512]{1,0:T(8,128)(2,1)S(1)} %get-tuple-element.150.refs_3_), channel_id=1, source_target_pairs={{0,1},{1,2},{2,3},{3,0},{4,5},{5,6},{6,7},{7,4},{8,9},{9,10},{10,1... | collective-permute-start | bytes 786440 | tf_op jit(solution)/shard_map/ppermute | solution.py:48
  133.5 4.0 %collective-permute-done.27.refs_5_ = bf16[256,512]{1,0:T(8,128)(2,1)S(1)} collective-permute-done((bf16[256,512]{1,0:T(8,128)(2,1)S(1)}, bf16[256,512]{1,0:T(8,128)(2,1)S(1)}, u32[]{:S(2)}, u32[]{:S(2)}) %collective-permute-start.27) | collective-permute-done | bytes 262176 | tf_op jit(solution)/shard_map/ppermute | solution.py:48
  140.8 7.5 %feed_up.1 = (bf16[512,2048]{1,0:T(8,128)(2,1)S(1)}, f32[512,1]{1,0:T(8,128)}, f32[512,1]{1,0:T(8,128)}, f32[512,512]{1,0:T(8,128)}, bf16[512,1024]{1,0:T(8,128)(2,1)S(1)}, /*index=5*/bf16[512,1024]{1,0:T(8,128)(2,1)S(1)}) custom-call(s32[8]{0:T(128)S(1)} %stack.35.refs_6_.refs_0_, bf16[4,512,512]{2,1,0:T(8,128)(2,1)} %get-tuple-element.120.refs_1_, ...), custom_call_target="tpu_custom_call" | custom-call | flops 12099999744 | tf_op jit(solution)/shard_map/feed_up/pallas_call | solution.py:192
  153.8 7.1 %back_feed.1 = (bf16[272,512]{1,0:T(8,128)(2,1)S(1)}, bf16[256,512]{1,0:T(8,128)(2,1)S(1)}, bf16[272,512]{1,0:T(8,128)(2,1)S(1)}, bf16[256,512]{1,0:T(8,128)(2,1...) custom-call(s32[8]{0:T(128)S(1)} %stack.35.refs_6_.refs_0_, ...), custom_call_target="tpu_custom_call" | custom-call | flops 7699999744 | tf_op jit(solution)/shard_map/back_feed/pallas_call | solution.py:192
  179.6 5.0 %all-to-all-start = ((bf16[4,256,2048]{2,1,0:T(8,128)(2,1)}), bf16[4,256,2048]{2,1,0:T(8,128)(2,1)}, u32[]{:S(2)}, u32[]{:S(2)}) async-start(bf16[4,256,2048]{2,1,0:T(8,128)(2,1)} %bitcast.45), calls=%async_computation.1 | async-start | bytes 8388608 | tf_op jit(solution)/shard_map/all_to_all | solution.py:892
  185.4 4.4 %norm_back2.1 = (f32[512,512]{1,0:T(8,128)}, f32[1,512]{1,0:T(1,128)S(1)}, bf16[256,512]{1,0:T(8,128)(2,1)S(1)}, bf16[256,512]{1,0:T(8,128)(2,1)S(1)}) custom-call(s32[8]{0:T(128)S(1)} %stack.35.refs_6_.refs_0_, f32[512,512]{1,0:T(8,128)} %get-tuple-element.158.refs_1_, f32[16,512]{1,0:T(8,128)S(1)} %get-tuple-element.159.refs_2_, ...), custom_call_target="tpu_custom_call" | custom-call | flops 109999996928 | tf_op jit(solution)/shard_map/norm_back2/pallas_call | solution.py:192
  209.2 7.0 %back_mix.1 = (bf16[512,2048]{1,0:T(8,128)(2,1)S(1)}, bf16[512,1024]{1,0:T(8,128)(2,1)}, bf16[512,1024]{1,0:T(8,128)(2,1)}, f32[256,512]{1,0:T(8,128)S(1)}, bf16[256,512]{1,0:T(8,128)(2,1)S(1)}) custom-call(s32[8]{0:T(128)S(1)} %stack.35.refs_6_.refs_0_, bf16[256,512]{1,0:T(8,128)(2,1)S(1)} %get-tuple-element.168.refs_1_, ...), custom_call_target="tpu_custom_call" | custom-call | flops 6600000000 | tf_op jit(solution)/shard_map/back_mix/pallas_call | solution.py:192
  218.9 5.9 %retain_back.1 = (bf16[512,512]{1,0:T(8,128)(2,1)}, f32[512,512]{1,0:T(8,128)}, f32[512,1024]{1,0:T(8,128)}) custom-call(s32[8]{0:T(128)S(1)} %stack.35.refs_6_.refs_0_, bf16[512,1024]{1,0:T(8,128)(2,1)} %get-tuple-element.178.refs_1_, bf16[512,1024]{1,0:T(8,128)(2,1)} %get-tuple-element.123.refs_3_.refs_2_.refs_4_, ...), custom_call_target="tpu_custom_call" | custom-call | flops 660000000 | tf_op jit(solution)/shard_map/retain_back/pallas_call | solution.py:192
  224.8 6.8 %mix_other.1.refs_2_ = bf16[1024,2560]{1,0:T(8,128)(2,1)} custom-call(bf16[1024,512]{1,0:T(8,128)(2,1)} %bitcast.50, bf16[1024,512]{1,0:T(8,128)(2,1)} %bitcast.46, bf16[512,1024]{1,0:T(8,128)(2,1)} %get-tuple-element.176.refs_2_, bf16[512,1024]{1,0:T(8,128)(2,1)} %get-tuple-element.177.refs_3_.refs_2_, ...), custom_call_target="tpu_custom_call" | custom-call | flops 198000000 | tf_op jit(solution)/shard_map/mix_other/pallas_call | solution.py:192
  241.0 7.5 %mix_own.1.refs_5_.refs_0_ = bf16[1024,2560]{1,0:T(8,128)(2,1)} custom-call(bf16[1024,512]{1,0:T(8,128)(2,1)} %bitcast.49, bf16[1024,512]{1,0:T(8,128)(2,1)} %bitcast.44, bf16[512,1024]{1,0:T(8,128)(2,1)} %get-tuple-element.176.refs_2_, bf16[512,1024]{1,0:T(8,128)(2,1)} %get-tuple-element.177.refs_3_.refs_2_, ...), custom_call_target="tpu_custom_call" | custom-call | flops 1100000000 | tf_op jit(solution)/shard_map/mix_own/pallas_call | solution.py:192
  268.2 5.2 %all-to-all-start.1 = ((bf16[4,256,2560]{2,1,0:T(8,128)(2,1)}), bf16[4,256,2560]{2,1,0:T(8,128)(2,1)}, u32[]{:S(2)}, u32[]{:S(2)}) async-start(bf16[4,256,2560]{2,1,0:T(8,128)(2,1)} %bitcast.42), calls=%async_computation.2 | async-start | bytes 10485760 | tf_op jit(solution)/shard_map/all_to_all | solution.py:892
  277.3 4.3 %key_value_back.1 = (bf16[512,512]{1,0:T(8,128)(2,1)}, bf16[512,1024]{1,0:T(8,128)(2,1)}) custom-call(s32[8]{0:T(128)S(1)} %stack.35.refs_6_.refs_0_, bf16[256,512]{1,0:T(8,128)(2,1)S(1)} %copy-done.18, bf16[256,512]{1,0:T(8,128)(2,1)S(1)} %collective-permute-done.56.refs_2_, bf16[512,512]{1,0:T(8,128)(2,1)} %get-tuple-element.122.refs_2_.refs_4_.refs_3_, ...), custom_call_target="tpu_custom_call" | custom-call | flops 109999996928 | tf_op jit(solution)/shard_map/key_value_back/pallas_call | solution.py:192
  281.6 4.9 %kv_other.1.refs_17_ = bf16[1024,1536]{1,0:T(8,128)(2,1)} custom-call(bf16[1024,512]{1,0:T(8,128)(2,1)} %bitcast.47, bf16[512,512]{1,0:T(8,128)(2,1)} %get-tuple-element.195.refs_1_.refs_3_, bf16[512,1024]{1,0:T(8,128)(2,1)} %get-tuple-element.196.refs_2_.refs_4_), custom_call_target="tpu_custom_call" | custom-call | flops 990000000 | tf_op jit(solution)/shard_map/kv_other/pallas_call | solution.py:192
  287.0 13.5 %back_proj.1 = (bf16[272,512]{1,0:T(8,128)(2,1)S(1)}, bf16[256,512]{1,0:T(8,128)(2,1)S(1)}, bf16[272,512]{1,0:T(8,128)(2,1)S(1)}, bf16[256,512]{1,0:T(8,128)(2,1...) custom-call(s32[8]{0:T(128)S(1)} %stack.35.refs_6_.refs_0_, ...), custom_call_target="tpu_custom_call" | custom-call | flops 110000000 | tf_op jit(solution)/shard_map/back_proj/pallas_call | solution.py:192
  307.0 4.3 %collective-permute-done.57 = bf16[272,512]{1,0:T(8,128)(2,1)S(1)} collective-permute-done((bf16[272,512]{1,0:T(8,128)(2,1)S(1)}, bf16[272,512]{1,0:T(8,128)(2,1)S(1)}, u32[]{:S(2)}, u32[]{:S(2)}) %collective-permute-start.57) | collective-permute-done | bytes 278560 | tf_op jit(solution)/shard_map/ppermute | solution.py:48
  314.8 7.1 %kv_own.1 = (bf16[256,1536]{1,0:T(8,128)(2,1)S(1)}, bf16[256,1536]{1,0:T(8,128)(2,1)}, bf16[256,1536]{1,0:T(8,128)(2,1)}, f32[256,1536]{1,0:T(8,128)S(1)}) custom-call(s32[8]{0:T(128)S(1)} %stack.35.refs_6_.refs_0_, bf16[4,4,64,512]{3,2,1,0:T(8,128)(2,1)} %get-tuple-element.148.refs_1_.refs_2_, bf16[4,4,64,512]{3,2,1,0:T(8,128)(2,1)} %get-tuple-element.148.refs_1_.refs_2_, ...), custom_call_target="tpu_custom_call" | custom-call | flops 110000000 | tf_op jit(solution)/shard_map/kv_own/pallas_call | solution.py:192
  343.2 4.3 %mix_mid.1 = bf16[4,64,3072]{2,1,0:T(8,128)(2,1)} custom-call(bf16[4,256,2560]{2,1,0:T(8,128)(2,1)} %all-to-all-done.1.refs_2_.refs_0_, f32[16,512]{1,0:T(8,128)S(1)} %pad.4.refs_1_), custom_call_target="tpu_custom_call" | custom-call | flops 110000000 | tf_op jit(solution)/shard_map/mix_mid/pallas_call | solution.py:192
  347.5 4.5 %all-to-all-start.2 = ((bf16[4,64,3072]{2,1,0:T(8,128)(2,1)}), bf16[4,64,3072]{2,1,0:T(8,128)(2,1)}, u32[]{:S(2)}, u32[]{:S(2)}) async-start(bf16[4,64,3072]{2,1,0:T(8,128)(2,1)} %mix_mid.1), calls=%async_computation.4 | async-start | bytes 3145728 | tf_op jit(solution)/shard_map/all_to_all | solution.py:892
  352.0 7.7 %collective-permute-done.69.refs_3_ = bf16[256,1536]{1,0:T(8,128)(2,1)} collective-permute-done((bf16[256,1536]{1,0:T(8,128)(2,1)}, bf16[256,1536]{1,0:T(8,128)(2,1)}, u32[]{:S(2)}, u32[]{:S(2)}) %collective-permute-start.69) | collective-permute-done | bytes 786464 | tf_op jit(solution)/shard_map/ppermute | solution.py:1053
  (310 shorter events, 221.3 us)
Async XLA Ops:
  8.3 20.5 %collective-permute-start.1 = (bf16[256,512]{1,0:T(8,128)(2,1)S(1)}, bf16[256,512]{1,0:T(8,128)(2,1)S(1)}, u32[]{:S(2)}, u32[]{:S(2)}) collective-permute-start(bf16[256,512]{1,0:T(8,128)(2,1)S(1)} %get-tuple-element.227.refs_2_), channel_id=1, source_target_pairs={{0,1},{1,2},{2,3},{3,0},{4,5},{5,6},{6,7},{7,4},{8,9},{9,10},{10,1... | collective-permute-start | bytes 786440 | tf_op jit(solution)/shard_map/ppermute | solution.py:48
  36.8 22.1 %collective-permute-start.7 = (bf16[512,512]{1,0:T(8,128)(2,1)S(1)}, bf16[512,512]{1,0:T(8,128)(2,1)S(1)}, u32[]{:S(2)}, u32[]{:S(2)}) collective-permute-start(bf16[512,512]{1,0:T(8,128)(2,1)S(1)} %get-tuple-element.129.refs_1_), channel_id=1, source_target_pairs={{0,1},{1,2},{2,3},{3,0},{4,5},{5,6},{6,7},{7,4},{8,9},{9,10},{10,1... | collective-permute-start | bytes 1572872 | tf_op jit(solution)/shard_map/ppermute | solution.py:95
  36.8 25.5 %collective-permute-start.8 = (bf16[512,512]{1,0:T(8,128)(2,1)S(1)}, bf16[512,512]{1,0:T(8,128)(2,1)S(1)}, u32[]{:S(2)}, u32[]{:S(2)}) collective-permute-start(bf16[512,512]{1,0:T(8,128)(2,1)S(1)} %get-tuple-element.129.refs_1_), channel_id=1, source_target_pairs={{0,2},{1,3},{2,0},{3,1},{4,6},{5,7},{6,4},{7,5},{8,10},{9,11},{10,... | collective-permute-start | bytes 1572872 | tf_op jit(solution)/shard_map/ppermute | solution.py:95
  41.2 21.1 %collective-permute-start.9 = (bf16[512,512]{1,0:T(8,128)(2,1)S(1)}, bf16[512,512]{1,0:T(8,128)(2,1)S(1)}, u32[]{:S(2)}, u32[]{:S(2)}) collective-permute-start(bf16[512,512]{1,0:T(8,128)(2,1)S(1)} %get-tuple-element.129.refs_1_), channel_id=1, source_target_pairs={{0,3},{1,0},{2,1},{3,2},{4,7},{5,4},{6,5},{7,6},{8,11},{9,8},{10,9... | collective-permute-start | bytes 1572872 | tf_op jit(solution)/shard_map/ppermute | solution.py:95
  97.4 16.6 %collective-permute-start.22 = (bf16[256,512]{1,0:T(8,128)(2,1)S(1)}, bf16[256,512]{1,0:T(8,128)(2,1)S(1)}, u32[]{:S(2)}, u32[]{:S(2)}) collective-permute-start(bf16[256,512]{1,0:T(8,128)(2,1)S(1)} %get-tuple-element.142), channel_id=1, source_target_pairs={{0,1},{1,2},{2,3},{3,0},{4,5},{5,6},{6,7},{7,4},{8,9},{9,10},{10,1... | collective-permute-start | bytes 786440 | tf_op jit(solution)/shard_map/ppermute | solution.py:48
  97.4 16.6 %collective-permute-start.23 = (bf16[256,512]{1,0:T(8,128)(2,1)S(1)}, bf16[256,512]{1,0:T(8,128)(2,1)S(1)}, u32[]{:S(2)}, u32[]{:S(2)}) collective-permute-start(bf16[256,512]{1,0:T(8,128)(2,1)S(1)} %get-tuple-element.143), channel_id=1, source_target_pairs={{0,3},{1,0},{2,1},{3,2},{4,7},{5,4},{6,5},{7,6},{8,11},{9,8},{10,9... | collective-permute-start | bytes 786440 | tf_op jit(solution)/shard_map/ppermute | solution.py:52
  118.5 19.0 %collective-permute-start.27 = (bf16[256,512]{1,0:T(8,128)(2,1)S(1)}, bf16[256,512]{1,0:T(8,128)(2,1)S(1)}, u32[]{:S(2)}, u32[]{:S(2)}) collective-permute-start(bf16[256,512]{1,0:T(8,128)(2,1)S(1)} %get-tuple-element.150.refs_3_), channel_id=1, source_target_pairs={{0,1},{1,2},{2,3},{3,0},{4,5},{5,6},{6,7},{7,4},{8,9},{9,10},{10,1... | collective-permute-start | bytes 786440 | tf_op jit(solution)/shard_map/ppermute | solution.py:48
  153.8 21.9 %collective-permute-start.38 = (bf16[1024,2048]{1,0:T(8,128)(2,1)}, bf16[1024,2048]{1,0:T(8,128)(2,1)S(1)}, u32[]{:S(2)}, u32[]{:S(2)}) collective-permute-start(bf16[1024,2048]{1,0:T(8,128)(2,1)} %feed_other.1.refs_8_), channel_id=1, source_target_pairs={{0,4},{4,0},{8,12},{12,8},{16,20},{20,16},{24,28},{28,24},{32,36},... | collective-permute-start | bytes 12582920 | tf_op jit(solution)/shard_map/ppermute | solution.py:1245
  163.8 20.8 %collective-permute-start.34 = (bf16[256,512]{1,0:T(8,128)(2,1)}, bf16[256,512]{1,0:T(8,128)(2,1)S(1)}, u32[]{:S(2)}, u32[]{:S(2)}) collective-permute-start(bf16[256,512]{1,0:T(8,128)(2,1)} %get-tuple-element.162), channel_id=1, source_target_pairs={{0,1},{1,2},{2,3},{3,0},{4,5},{5,6},{6,7},{7,4},{8,9},{9,10},{10,1... | collective-permute-start | bytes 786440 | tf_op jit(solution)/shard_map/ppermute | solution.py:48
  163.8 20.8 %collective-permute-start.35 = (bf16[272,512]{1,0:T(8,128)(2,1)S(1)}, bf16[272,512]{1,0:T(8,128)(2,1)S(1)}, u32[]{:S(2)}, u32[]{:S(2)}) collective-permute-start(bf16[272,512]{1,0:T(8,128)(2,1)S(1)} %get-tuple-element.163), channel_id=1, source_target_pairs={{0,3},{1,0},{2,1},{3,2},{4,7},{5,4},{6,5},{7,6},{8,11},{9,8},{10,9... | collective-permute-start | bytes 835592 | tf_op jit(solution)/shard_map/ppermute | solution.py:52
  179.6 56.4 %all-to-all-start = ((bf16[4,256,2048]{2,1,0:T(8,128)(2,1)}), bf16[4,256,2048]{2,1,0:T(8,128)(2,1)}, u32[]{:S(2)}, u32[]{:S(2)}) async-start(bf16[4,256,2048]{2,1,0:T(8,128)(2,1)} %bitcast.45), calls=%async_computation.1 | async-start | bytes 8388608 | tf_op jit(solution)/shard_map/all_to_all | solution.py:892
  184.6 81.8 %reduce-scatter.3.cloned.1.call-start = ((), (), s32[]{:S(2)}) async-start(), calls=%async_computation.5 | async-start | bytes 2621440 | tf_op jit(solution)/shard_map/reduce_scatter | solution.py:1283
  216.3 19.7 %collective-permute-start.45 = (bf16[256,512]{1,0:T(8,128)(2,1)S(1)}, bf16[256,512]{1,0:T(8,128)(2,1)S(1)}, u32[]{:S(2)}, u32[]{:S(2)}) collective-permute-start(bf16[256,512]{1,0:T(8,128)(2,1)S(1)} %get-tuple-element.173.refs_2_), channel_id=1, source_target_pairs={{0,4},{4,0},{8,12},{12,8},{16,20},{20,16},{24,28},{28,24},{32,36},... | collective-permute-start | bytes 786440 | tf_op jit(solution)/shard_map/ppermute | solution.py:1098
  268.2 66.3 %all-to-all-start.1 = ((bf16[4,256,2560]{2,1,0:T(8,128)(2,1)}), bf16[4,256,2560]{2,1,0:T(8,128)(2,1)}, u32[]{:S(2)}, u32[]{:S(2)}) async-start(bf16[4,256,2560]{2,1,0:T(8,128)(2,1)} %bitcast.42), calls=%async_computation.2 | async-start | bytes 10485760 | tf_op jit(solution)/shard_map/all_to_all | solution.py:892
  273.4 58.7 %reduce-scatter.5.cloned.1.call-start = ((), (), s32[]{:S(2)}) async-start(), calls=%async_computation.6 | async-start | bytes 1310720 | tf_op jit(solution)/shard_map/reduce_scatter | solution.py:1292
  286.4 28.4 %collective-permute-start.63 = (bf16[1024,1536]{1,0:T(8,128)(2,1)}, bf16[1024,1536]{1,0:T(8,128)(2,1)}, u32[]{:S(2)}, u32[]{:S(2)}) collective-permute-start(bf16[1024,1536]{1,0:T(8,128)(2,1)} %kv_other.1.refs_17_), channel_id=1, source_target_pairs={{0,4},{4,0},{8,12},{12,8},{16,20},{20,16},{24,28},{28,24},{32,36},... | collective-permute-start | bytes 9437192 | tf_op jit(solution)/shard_map/ppermute | solution.py:1303
  303.8 21.0 %collective-permute-start.59 = (bf16[256,512]{1,0:T(8,128)(2,1)S(1)}, bf16[256,512]{1,0:T(8,128)(2,1)S(1)}, u32[]{:S(2)}, u32[]{:S(2)}) collective-permute-start(bf16[256,512]{1,0:T(8,128)(2,1)S(1)} %get-tuple-element.201), channel_id=1, source_target_pairs={{0,1},{1,2},{2,3},{3,0},{4,5},{5,6},{6,7},{7,4},{8,9},{9,10},{10,1... | collective-permute-start | bytes 786440 | tf_op jit(solution)/shard_map/ppermute | solution.py:48
  303.8 21.6 %collective-permute-start.60 = (bf16[272,512]{1,0:T(8,128)(2,1)S(1)}, bf16[272,512]{1,0:T(8,128)(2,1)S(1)}, u32[]{:S(2)}, u32[]{:S(2)}) collective-permute-start(bf16[272,512]{1,0:T(8,128)(2,1)S(1)} %get-tuple-element.202), channel_id=1, source_target_pairs={{0,3},{1,0},{2,1},{3,2},{4,7},{5,4},{6,5},{7,6},{8,11},{9,8},{10,9... | collective-permute-start | bytes 835592 | tf_op jit(solution)/shard_map/ppermute | solution.py:52
  311.3 16.6 %collective-permute-start.58 = (bf16[272,512]{1,0:T(8,128)(2,1)S(1)}, bf16[272,512]{1,0:T(8,128)(2,1)S(1)}, u32[]{:S(2)}, u32[]{:S(2)}) collective-permute-start(bf16[272,512]{1,0:T(8,128)(2,1)S(1)} %add_convert_fusion.1.refs_7_), channel_id=1, source_target_pairs={{0,1},{1,2},{2,3},{3,0},{4,5},{5,6},{6,7},{7,4},{8,9},{9,10},{10,1... | collective-permute-start | bytes 835592 | tf_op jit(solution)/shard_map/ppermute | solution.py:48
  311.5 16.5 %collective-permute-start.62 = (bf16[256,512]{1,0:T(8,128)(2,1)S(1)}, bf16[256,512]{1,0:T(8,128)(2,1)S(1)}, u32[]{:S(2)}, u32[]{:S(2)}) collective-permute-start(bf16[256,512]{1,0:T(8,128)(2,1)S(1)} %add_convert_fusion.3.refs_8_), channel_id=1, source_target_pairs={{0,3},{1,0},{2,1},{3,2},{4,7},{5,4},{6,5},{7,6},{8,11},{9,8},{10,9... | collective-permute-start | bytes 786440 | tf_op jit(solution)/shard_map/ppermute | solution.py:52
  321.9 30.1 %collective-permute-start.68 = (bf16[256,1536]{1,0:T(8,128)(2,1)S(1)}, bf16[256,1536]{1,0:T(8,128)(2,1)S(1)}, u32[]{:S(2)}, u32[]{:S(2)}) collective-permute-start(bf16[256,1536]{1,0:T(8,128)(2,1)S(1)} %get-tuple-element.208.refs_12_), channel_id=1, source_target_pairs={{0,16},{4,20},{8,24},{12,28},{16,0},{20,4},{24,8},{28,12},{32,48},... | collective-permute-start | bytes 2359304 | tf_op jit(solution)/shard_map/ppermute | solution.py:1053
  324.7 35.0 %collective-permute-start.69 = (bf16[256,1536]{1,0:T(8,128)(2,1)}, bf16[256,1536]{1,0:T(8,128)(2,1)}, u32[]{:S(2)}, u32[]{:S(2)}) collective-permute-start(bf16[256,1536]{1,0:T(8,128)(2,1)} %get-tuple-element.215), channel_id=1, source_target_pairs={{0,8},{4,12},{8,16},{12,20},{16,24},{20,28},{24,0},{28,4},{32,40},... | collective-permute-start | bytes 2359304 | tf_op jit(solution)/shard_map/ppermute | solution.py:1053
  325.3 35.4 %collective-permute-start.70 = (bf16[256,1536]{1,0:T(8,128)(2,1)}, bf16[256,1536]{1,0:T(8,128)(2,1)}, u32[]{:S(2)}, u32[]{:S(2)}) collective-permute-start(bf16[256,1536]{1,0:T(8,128)(2,1)} %get-tuple-element.216), channel_id=1, source_target_pairs={{0,24},{4,28},{8,0},{12,4},{16,8},{20,12},{24,16},{28,20},{32,56},... | collective-permute-start | bytes 2359304 | tf_op jit(solution)/shard_map/ppermute | solution.py:1053
  347.5 27.2 %all-to-all-start.2 = ((bf16[4,64,3072]{2,1,0:T(8,128)(2,1)}), bf16[4,64,3072]{2,1,0:T(8,128)(2,1)}, u32[]{:S(2)}, u32[]{:S(2)}) async-start(bf16[4,64,3072]{2,1,0:T(8,128)(2,1)} %mix_mid.1), calls=%async_computation.4 | async-start | bytes 3145728 | tf_op jit(solution)/shard_map/all_to_all | solution.py:892
  (97 other events, 1071.2 us)
Sparse Core Ops, SparseCore 0:
  236.1 30.2 reduce-scatter.2
  287.1 24.0 reduce-scatter.4
